TPU v7x, 256 devices: a whole 4x4x8 slice. The times are simulated.
256 devices in a mesh: seq: 32 (over x, z), dp: 8 (over y, core).
Axes of the slice: x: 4, y: 4, z: 8, core: 2. Of those that a mesh axis runs over, the one named last changes fastest.
Arguments:
- token_ids: int32 [8, 4096], P('dp', 'seq'), may hold values from 0 to 511
- embedding: bfloat16 [512, 2048], replicated, may hold values from -6 to 6
- short_taps: float32 [3, 3, 2048], replicated, may hold values from -3 to 3
- long_filter: float32 [2048, 4096], P('seq'), may hold values from -0.09375 to 0.09375
- skip_gain: float32 [2048], P('seq'), may hold values from -4 to 4
- out_cotangent: bfloat16 [8, 2048, 4096], P('dp', None, 'seq'), may hold values from -0.032958984 to 0.032958984
Outputs:
- out: bfloat16 [8, 2048, 4096], P('dp', None, 'seq')
- grad_filter: float32 [2048, 4096], P(('seq', 'dp'))
- grad_skip: float32 [2048], P(('seq', 'dp'))
- grad_taps: float32 [3, 3, 2048], replicated
All inputs are finite; a program needn't handle non-finite values.
Results may differ from a plain program's by a relative error of at most 0.04.
Values may be sent and summed in bfloat16 or wider, within the bound.
A program may use at most 128 MiB of HBM per device.

v0:
```python
import math

import jax
import jax.numpy as jnp
from jax import lax
from jax.sharding import PartitionSpec as P

STREAMS = 3
TAPS = 3
FFT_COLS = 128


def shifted(block, axis, distance):
    devices = range(lax.axis_size(axis))
    route = [(i - distance, i) for i in devices if i - distance in devices]
    return lax.ppermute(block, axis, route)


def unit_table(first_len, second_len, modulus):
    first_index = lax.broadcasted_iota(jnp.int32, (first_len, second_len), 0)
    second_index = lax.broadcasted_iota(jnp.int32, (first_len, second_len), 1)
    phase = first_index * second_index % modulus
    angle = phase.astype(jnp.float32) * (2.0 * math.pi / modulus)
    return (jnp.cos(angle), jnp.sin(angle))


def contract(form, left, right):
    return jnp.einsum(form, left, right, precision=lax.Precision.HIGH)


def forward_transform(signal):
    channels, length = signal.shape
    total = 2 * length
    rows = total // FFT_COLS
    half = rows // 2
    grid = signal.astype(jnp.float32).reshape(channels, half, FFT_COLS)
    row_cos, row_sin = unit_table(half, rows, rows)
    row_both = jnp.concatenate([row_cos, -row_sin], axis=1)
    first = contract("cnm,nk->ckm", grid, row_both)
    first_re = first[:, :rows]
    first_im = first[:, rows:]
    twist_cos, twist_sin = unit_table(rows, FFT_COLS, total)
    turned_re = first_re * twist_cos + first_im * twist_sin
    turned_im = first_im * twist_cos - first_re * twist_sin
    turned = jnp.concatenate([turned_re, turned_im], axis=2)
    col_cos, col_sin = unit_table(FFT_COLS, FFT_COLS, FFT_COLS)
    col_both = jnp.concatenate(
        [jnp.concatenate([col_cos, -col_sin], axis=1), jnp.concatenate([col_sin, col_cos], axis=1)],
        axis=0,
    )
    spectrum = contract("ckm,mj->ckj", turned, col_both)
    return (spectrum[:, :, :FFT_COLS], spectrum[:, :, FFT_COLS:])


def inverse_transform(spec_re, spec_im):
    channels, rows, cols = spec_re.shape
    total = rows * cols
    half = rows // 2
    merged = jnp.concatenate([spec_re, spec_im], axis=2)
    col_cos, col_sin = unit_table(cols, cols, cols)
    col_both = jnp.concatenate(
        [jnp.concatenate([col_cos, col_sin], axis=1), jnp.concatenate([-col_sin, col_cos], axis=1)],
        axis=0,
    )
    back = contract("ckj,jm->ckm", merged, col_both)
    back_re = back[:, :, :cols]
    back_im = back[:, :, cols:]
    twist_cos, twist_sin = unit_table(rows, cols, total)
    turned_re = back_re * twist_cos - back_im * twist_sin
    turned_im = back_im * twist_cos + back_re * twist_sin
    stacked = jnp.concatenate([turned_re, turned_im], axis=1)
    row_cos, row_sin = unit_table(rows, half, rows)
    row_both = jnp.concatenate([row_cos, -row_sin], axis=0)
    signal = contract("ckm,kn->cnm", stacked, row_both)
    return signal.reshape(channels, half * cols) * (1.0 / total)


def make_streams(taps, embedded, previous):
    length = embedded.shape[1]
    extended = jnp.concatenate([previous, embedded], axis=1).astype(jnp.float32)
    lagged = [extended[:, TAPS - 1 - lag : TAPS - 1 - lag + length] for lag in range(TAPS)]
    streams = []
    for stream in range(STREAMS):
        summed = taps[stream, 0][:, None] * lagged[0]
        for lag in range(1, TAPS):
            summed = summed + taps[stream, lag][:, None] * lagged[lag]
        streams.append(summed.astype(jnp.bfloat16).astype(jnp.float32))
    return (lagged, streams[0], streams[1], streams[2])


def spectral(
    gated_ch, back_ch, gated_re, gated_im, back_re, back_im, filter_re, filter_im, skip_gain
):
    gated_chf = gated_ch.astype(jnp.float32)
    back_chf = back_ch.astype(jnp.float32)
    conv = inverse_transform(
        gated_re * filter_re - gated_im * filter_im, gated_re * filter_im + gated_im * filter_re
    )
    response_ch = (conv + skip_gain[:, None] * gated_chf).astype(jnp.bfloat16)
    corr = inverse_transform(
        back_re * filter_re + back_im * filter_im, back_im * filter_re - back_re * filter_im
    )
    grad_ch = (corr + skip_gain[:, None] * back_chf).astype(jnp.bfloat16)
    skip_local = jnp.sum(back_chf * gated_chf, axis=1)
    term_re = gated_re * back_re + gated_im * back_im
    term_im = gated_re * back_im - gated_im * back_re
    return (response_ch, grad_ch, skip_local, term_re, term_im)


def tap_terms(grads, lagged):
    return jnp.stack(
        [
            jnp.stack([jnp.sum(grad_one * lagged[lag], axis=1) for lag in range(TAPS)])
            for grad_one in grads
        ]
    )


def shards(token_ids, embedding, short_taps, long_filter, skip_gain, out_cotangent):
    token_row = token_ids[0]
    cotangent = out_cotangent[0]
    width, local_len = cotangent.shape
    seq_count = lax.axis_size("seq")
    own_channels = width // seq_count
    vocab_rows = embedding.shape[0]
    filter_re, filter_im = forward_transform(long_filter)
    onehot = (
        lax.broadcasted_iota(jnp.int32, (vocab_rows, local_len), 0) == token_row[None, :]
    ).astype(jnp.bfloat16)
    embedded = jnp.einsum(
        "vd,vp->dp", embedding, onehot, preferred_element_type=jnp.float32
    ).astype(jnp.bfloat16)
    previous = shifted(embedded[:, local_len - (TAPS - 1) :], "seq", 1)
    lagged, first_f, second_f, value_f = make_streams(short_taps, embedded, previous)
    cot_f = cotangent.astype(jnp.float32)
    gated = (first_f * value_f).astype(jnp.bfloat16)
    back_signal = (cot_f * second_f).astype(jnp.bfloat16)
    shaped = (
        gated.reshape(seq_count, own_channels, local_len),
        back_signal.reshape(seq_count, own_channels, local_len),
    )
    gated_part = lax.all_to_all(shaped[0], "seq", split_axis=0, concat_axis=2, tiled=True)[0]
    back_part = lax.all_to_all(shaped[1], "seq", split_axis=0, concat_axis=2, tiled=True)[0]
    gated_re, gated_im = forward_transform(gated_part)
    back_re, back_im = forward_transform(back_part)
    gated_ch, back_ch, gated_re, gated_im, back_re, back_im = (
        gated_part,
        back_part,
        gated_re,
        gated_im,
        back_re,
        back_im,
    )
    response_ch, grad_ch, skip_local, term_re, term_im = spectral(
        gated_ch, back_ch, gated_re, gated_im, back_re, back_im, filter_re, filter_im, skip_gain
    )
    returned = (
        lax.all_to_all(
            response_ch.reshape(own_channels, seq_count, local_len),
            "seq",
            split_axis=1,
            concat_axis=0,
            tiled=True,
        ),
        lax.all_to_all(
            grad_ch.reshape(own_channels, seq_count, local_len),
            "seq",
            split_axis=1,
            concat_axis=0,
            tiled=True,
        ),
    )
    response_f = returned[0].reshape(width, local_len).astype(jnp.float32)
    grad_gated_f = returned[1].reshape(width, local_len).astype(jnp.float32)
    out = (second_f * response_f).astype(jnp.bfloat16)
    grads = [grad_gated_f * value_f, cot_f * response_f, grad_gated_f * first_f]
    tap_local = tap_terms(grads, lagged)
    filter_local = inverse_transform(term_re, term_im)
    grad_filter, grad_skip = (
        lax.psum_scatter(filter_local, "dp", scatter_dimension=0, tiled=True),
        lax.psum_scatter(skip_local, "dp", scatter_dimension=0, tiled=True),
    )
    grad_taps = lax.psum(tap_local, ("seq", "dp"))
    return (out[None], grad_filter, grad_skip, grad_taps)


def solution(mesh):
    return jax.shard_map(
        shards,
        mesh=mesh,
        in_specs=(P("dp", "seq"), P(), P(), P("seq", None), P("seq"), P("dp", None, "seq")),
        out_specs=(P("dp", None, "seq"), P(("seq", "dp"), None), P(("seq", "dp")), P()),
        check_vma=False,
    )
```

profile of v0, /device:TPU:1, one launch (start us, length us, event | category | flops | bytes accessed | tf_op | source)
XLA Modules:
  0.0 403.4 jit_solution(17922813255601750739)
XLA Ops:
  10.8 4.4 %collective-permute-start = (bf16[2048,2]{0,1:T(2,128)(2,1)S(1)}, bf16[2048,2]{0,1:T(2,128)(2,1)S(1)}, u32[]{:S(2)}, u32[]{:S(2)}) collective-permute-start(bf16[2048,2]{0,1:T(2,128)(2,1)S(1)} %slice.124), channel_id=1, source_target_pairs={{0,8},{8,16},{16,24},{24,32},{32,40},{40,48},{48,56},{56,64},{64,7... | collective-permute-start | bytes 24584 | tf_op jit(solution)/shard_map/ppermute | solution.py:16
  19.0 12.3 %all-to-all-start.2 = ((bf16[32,64,128]{2,1,0:T(8,128)(2,1)}), bf16[32,64,128]{2,1,0:T(8,128)(2,1)S(1)}, u32[]{:S(2)}, u32[]{:S(2)}) async-start(bf16[32,64,128]{2,1,0:T(8,128)(2,1)} %bitcast.125), calls=%async_computation.2 | async-start | bytes 1048576 | tf_op jit(solution)/shard_map/all_to_all | solution.py:143
  35.0 9.3 %all-to-all-done.2 = bf16[32,64,128]{2,1,0:T(8,128)(2,1)S(1)} async-done(((bf16[32,64,128]{2,1,0:T(8,128)(2,1)}), bf16[32,64,128]{2,1,0:T(8,128)(2,1)S(1)}, u32[]{:S(2)}, u32[]{:S(2)}) %all-to-all-start.2) | async-done | bytes 524320 | tf_op jit(solution)/shard_map/all_to_all | solution.py:143
  44.3 7.6 %all-to-all-start = ((bf16[32,64,128]{2,1,0:T(8,128)(2,1)}), bf16[32,64,128]{2,1,0:T(8,128)(2,1)S(1)}, u32[]{:S(2)}, u32[]{:S(2)}) async-start(bf16[32,64,128]{2,1,0:T(8,128)(2,1)} %bitcast.124), calls=%async_computation | async-start | bytes 1048576 | tf_op jit(solution)/shard_map/all_to_all | solution.py:142
  52.5 5.1 %convolution_bitcast_fusion.1 = f32[64,128,128]{2,1,0:T(8,128)} fusion(f32[64,32,128]{2,1,0:T(8,128)} %bitcast.119, f32[32,64]{1,0:T(8,128)S(1)} %get-tuple-element.77, f32[32,64]{1,0:T(8,128)S(1)} %get-tuple-element.78), kind=kOutput, calls=%fused_computation.39 | convolution fusion | flops 201330688 | bytes 5259264 | tf_op jit(solution)/shard_map/cnm,nk->ckm/dot_general | solution.py:28
  57.6 3.3 convolution_bitcast_fusion
  60.9 3.3 all-to-all-done
  66.4 3.9 multiply_add_fusion.4
  72.1 3.7 fusion.4
  77.6 2.6 multiply_add_fusion.3
  80.3 6.2 %multiply_add_fusion.1 = (f32[64,64,128]{2,1,0:T(8,128)}, f32[64,64,128]{2,1,0:T(8,128)}, f32[64,64,128]{2,1,0:T(8,128)S(1)}, f32[64,64,128]{2,1,0:T(8,128)}) fusion(f32[64,64,256]{2,1,0:T(8,128)S(1)} %fusion.16, f32[64,64,256]{2,1,0:T(8,128)} %fusion.4, f32[64,64,256]{2,1,0:T(8,128)S(1)} %fusion), kind=kLoop, calls=%fused_computation.44 | loop fusion | flops 6291456 | bytes 20971520 | tf_op jit(solution)/shard_map/add | solution.py:101
  86.4 4.3 %fusion.28 = f32[64,64,256]{2,1,0:T(8,128)S(1)} fusion(f32[64,64,128]{2,1,0:T(8,128)} %get-tuple-element.37, f32[64,64,128]{2,1,0:T(8,128)} %get-tuple-element.36, f32[128,128]{1,0:T(8,128)S(1)} %get-tuple-element.82, f32[128,128]{1,0:T(8,128)S(1)} %fusion.97, f32[128,128]{1,0:T(8,128)S(1)} %get-tuple-element.81), kind=kOutput, calls=%fused_computation.28 | convolution fusion | flops 1611857920 | bytes 8585216 | tf_op jit(solution)/shard_map/ckj,jm->ckm/dot_general | solution.py:28
  95.1 4.2 %multiply_subtract_fusion = (f32[64,64,128]{2,1,0:T(8,128)S(1)}, f32[64,64,128]{2,1,0:T(8,128)S(1)}, f32[64,64,128]{2,1,0:T(8,128)}, f32[64,64,128]{2,1,0:T(8,12...) fusion(f32[64,64,256]{2,1,0:T(8,128)S(1)} %fusion.28, f32[64,128]{1,0:T(8,128)S(1)} %get-tuple-element.79, ...), kind=kLoop, calls=%fused_computation.42 | loop fusion | flops 9437184 | bytes 25231360 | tf_op jit(solution)/shard_map/sub | solution.py:69
  102.1 7.9 %all-to-all-start.3 = ((bf16[64,32,128]{2,0,1:T(8,128)(2,1)}), bf16[64,32,128]{2,0,1:T(8,128)(2,1)}, u32[]{:S(2)}, u32[]{:S(2)}) async-start(bf16[64,32,128]{2,0,1:T(8,128)(2,1)} %copy.35), calls=%async_computation.4 | async-start | bytes 1048576 | tf_op jit(solution)/shard_map/all_to_all | solution.py:165
  110.0 3.8 fusion.58
  114.8 7.0 %all-to-all-done.3 = bf16[64,32,128]{2,0,1:T(8,128)(2,1)} async-done(((bf16[64,32,128]{2,0,1:T(8,128)(2,1)}), bf16[64,32,128]{2,0,1:T(8,128)(2,1)}, u32[]{:S(2)}, u32[]{:S(2)}) %all-to-all-start.3) | async-done | bytes 524320 | tf_op jit(solution)/shard_map/all_to_all | solution.py:165
  121.8 7.7 %all-to-all-start.1 = ((bf16[64,32,128]{2,0,1:T(8,128)(2,1)}), bf16[64,32,128]{2,0,1:T(8,128)(2,1)}, u32[]{:S(2)}, u32[]{:S(2)}) async-start(bf16[64,32,128]{2,0,1:T(8,128)(2,1)} %copy.30), calls=%async_computation.1 | async-start | bytes 1048576 | tf_op jit(solution)/shard_map/all_to_all | solution.py:158
  131.7 2.5 copy.36
  134.2 6.6 %all-to-all-done.1 = bf16[64,32,128]{2,0,1:T(8,128)(2,1)} async-done(((bf16[64,32,128]{2,0,1:T(8,128)(2,1)}), bf16[64,32,128]{2,0,1:T(8,128)(2,1)}, u32[]{:S(2)}, u32[]{:S(2)}) %all-to-all-start.1) | async-done | bytes 524320 | tf_op jit(solution)/shard_map/all_to_all | solution.py:158
  143.0 2.6 copy.31
  145.5 3.8 multiply_reduce_fusion.8
  150.2 3.5 fusion.46
  157.9 19.0 %all-reduce = f32[64]{0:T(128)S(1)} all-reduce(f32[64]{0:T(128)S(1)} %multiply_reduce_fusion.9), channel_id=3, replica_groups=mesh['seq'=32,'dp'=8] {'dp'}, use_global_device_ids=true, to_apply=%region_2.3.clone | all-reduce | flops 64 | bytes 512
  179.6 214.8 %all-reduce.3.cloned.1.call-done = f32[3,3,2048]{2,1,0:T(4,128)} async-done(((f32[3,3,2048]{2,1,0:T(4,128)}), f32[3,3,2048]{2,1,0:T(4,128)}) %all-reduce.3.cloned.1.call-update) | async-done | bytes 73744 | tf_op jit(solution)/shard_map/psum | solution.py:183
  (60 shorter events, 37.7 us)
Async XLA Ops:
  8.0 1.6 copy-start
  8.0 7.1 %copy-start.7 = (f32[3,3,2048]{2,1,0:T(4,128)S(1)}, f32[3,3,2048]{2,1,0:T(4,128)}, u32[]{:S(2)}) copy-start(f32[3,3,2048]{2,1,0:T(4,128)} %param.8) | copy-start | bytes 221188
  8.0 7.2 %copy-start.6 = (bf16[1,2048,128]{2,1,0:T(8,128)(2,1)S(1)}, bf16[1,2048,128]{2,1,0:T(8,128)(2,1)}, u32[]{:S(2)}) copy-start(bf16[1,2048,128]{2,1,0:T(8,128)(2,1)} %param.11) | copy-start | bytes 1572868
  10.8 5.2 %collective-permute-start = (bf16[2048,2]{0,1:T(2,128)(2,1)S(1)}, bf16[2048,2]{0,1:T(2,128)(2,1)S(1)}, u32[]{:S(2)}, u32[]{:S(2)}) collective-permute-start(bf16[2048,2]{0,1:T(2,128)(2,1)S(1)} %slice.124), channel_id=1, source_target_pairs={{0,8},{8,16},{16,24},{24,32},{32,40},{40,48},{48,56},{56,64},{64,7... | collective-permute-start | bytes 24584 | tf_op jit(solution)/shard_map/ppermute | solution.py:16
  19.0 25.3 %all-to-all-start.2 = ((bf16[32,64,128]{2,1,0:T(8,128)(2,1)}), bf16[32,64,128]{2,1,0:T(8,128)(2,1)S(1)}, u32[]{:S(2)}, u32[]{:S(2)}) async-start(bf16[32,64,128]{2,1,0:T(8,128)(2,1)} %bitcast.125), calls=%async_computation.2 | async-start | bytes 1048576 | tf_op jit(solution)/shard_map/all_to_all | solution.py:143
  44.3 19.9 %all-to-all-start = ((bf16[32,64,128]{2,1,0:T(8,128)(2,1)}), bf16[32,64,128]{2,1,0:T(8,128)(2,1)S(1)}, u32[]{:S(2)}, u32[]{:S(2)}) async-start(bf16[32,64,128]{2,1,0:T(8,128)(2,1)} %bitcast.124), calls=%async_computation | async-start | bytes 1048576 | tf_op jit(solution)/shard_map/all_to_all | solution.py:142
  64.2 2.2 copy-start.2
  86.4 4.3 %copy-start.3 = (f32[64,64,128]{2,1,0:T(8,128)S(1)}, f32[64,64,128]{2,1,0:T(8,128)}, u32[]{:S(2)}) copy-start(f32[64,64,128]{2,1,0:T(8,128)} %get-tuple-element.55) | copy-start | bytes 6291460
  90.7 2.0 copy-start.4
  90.7 2.2 copy-start.5
  95.1 4.2 %copy-start.8 = (f32[64]{0:T(128)S(1)}, f32[64]{0:T(128)}, u32[]{:S(2)}) copy-start(f32[64]{0:T(128)} %param.10) | copy-start | bytes 772
  102.1 19.7 %all-to-all-start.3 = ((bf16[64,32,128]{2,0,1:T(8,128)(2,1)}), bf16[64,32,128]{2,0,1:T(8,128)(2,1)}, u32[]{:S(2)}, u32[]{:S(2)}) async-start(bf16[64,32,128]{2,0,1:T(8,128)(2,1)} %copy.35), calls=%async_computation.4 | async-start | bytes 1048576 | tf_op jit(solution)/shard_map/all_to_all | solution.py:165
  121.8 19.0 %all-to-all-start.1 = ((bf16[64,32,128]{2,0,1:T(8,128)(2,1)}), bf16[64,32,128]{2,0,1:T(8,128)(2,1)}, u32[]{:S(2)}, u32[]{:S(2)}) async-start(bf16[64,32,128]{2,0,1:T(8,128)(2,1)} %copy.30), calls=%async_computation.1 | async-start | bytes 1048576 | tf_op jit(solution)/shard_map/all_to_all | solution.py:158
  129.5 264.9 %all-reduce.3.cloned.1.call-start = ((), (), s32[]{:S(2)}) async-start(), calls=%async_computation.6 | async-start | bytes 196608 | tf_op jit(solution)/shard_map/psum | solution.py:183
  150.2 244.2 %reduce-scatter.2.cloned.1.call-start = ((), (), s32[]{:S(2)}) async-start(), calls=%async_computation.5 | async-start | bytes 1179648 | tf_op jit(solution)/shard_map/reduce_scatter | solution.py:180
  153.8 1.7 copy-start.9
  153.8 242.1 %copy-start.1 = (bf16[512,2048]{1,0:T(8,128)(2,1)S(1)}, bf16[512,2048]{1,0:T(8,128)(2,1)}, u32[]{:S(2)}) copy-start(bf16[512,2048]{1,0:T(8,128)(2,1)} %param.7) | copy-start | bytes 6291460
Sparse Core Ops, SparseCore 0:
  150.3 244.0 all-reduce.2
Sparse Core Ops, SparseCore 1:
  155.5 35.5 reduce-scatter.1
where the time goes:
time: 404 us; the launch traced here: 403 us
  waiting for transfers between devices  241 us (60%)
  starting transfers between devices  39.9 us (10%)
  matrix products  35.7 us (9%)
  other arithmetic  30 us (7%)
  local copies, waits for them, and re-layouts  21 us (5%)
  blocking collectives  19 us (5%)
  between operations  16.4 us (4%)
    psum x1, waiting for transfers between devices, shards(): grad_taps = lax.psum(tap_local, ('seq', 'dp'))  215 us
    dot_general x12, matrix products, contract(): return jnp.einsum(form, left, right, precision=lax.Precision.HIGH)  34.5 us
    unnamed x1, blocking collectives  19 us
    all_to_all x1, starting transfers between devices, shards(): lax.all_to_all(shaped[1], 'seq', split_axis=0, concat_axis=2, tiled=True)[0]  12.3 us
    unnamed x27, local copies, waits for them, and re-layouts  11.6 us
    all_to_all x1, waiting for transfers between devices, shards(): lax.all_to_all(shaped[1], 'seq', split_axis=0, concat_axis=2, tiled=True)[0]  9.28 us
  transfers between devices with their start and end apart: 7, of which 6 were waited for; matrix products, arithmetic and copies ran while one was open for 8% of the time, Pallas kernels for 0%

commit v1 on v0

v1 whole, which is shorter than its diff:
```python
import functools
import math

import jax
import jax.numpy as jnp
import ml_dtypes
import numpy as np
from jax import lax
from jax.experimental import pallas as pl
from jax.experimental.pallas import tpu as pltpu
from jax.sharding import PartitionSpec as P

MESH = pl.DeviceIdType.MESH
LANES = 128
F32 = jnp.float32
BF16 = jnp.bfloat16


def add(a, b):
    if a is None:
        return b
    if b is None:
        return a
    return a + b


def sub(a, b):
    if b is None:
        return a
    if a is None:
        return -b
    return a - b


def scale(a, factor):
    return None if a is None else a * factor


def neg(a):
    return None if a is None else -a


def turn(value, index, modulus, sign):
    re, im = value
    index %= modulus
    if index == 0:
        return value
    if 2 * index == modulus:
        return (neg(re), neg(im))
    if 4 * index == modulus:
        return (neg(im), re) if sign > 0 else (im, neg(re))
    if 4 * index == 3 * modulus:
        return (im, neg(re)) if sign > 0 else (neg(im), re)
    cos = math.cos(2 * math.pi * index / modulus)
    sin = sign * math.sin(2 * math.pi * index / modulus)
    if 8 * index % modulus == 0 and re is not None and im is not None:
        root = abs(cos)
        a, b = (re if cos > 0 else -re), (im if cos > 0 else -im)
        if (cos > 0) == (sin > 0):
            return ((a - b) * root, (a + b) * root)
        return ((a + b) * root, (b - a) * root)
    return (sub(scale(re, cos), scale(im, sin)), add(scale(re, sin), scale(im, cos)))


def complex_dft(values, sign):
    count = len(values)
    if count == 1:
        return values
    half = count // 2
    if count >= 4 and count % 4 == 0:
        quarter = count // 4
        parts = [complex_dft(values[r::4], sign) for r in range(4)]
        result = [None] * count
        for k in range(quarter):
            a, b, c, d = [turn(parts[r][k], r * k, count, sign) for r in range(4)]
            ac = (add(a[0], c[0]), add(a[1], c[1]))
            am = (sub(a[0], c[0]), sub(a[1], c[1]))
            bd = (add(b[0], d[0]), add(b[1], d[1]))
            bm = turn((sub(b[0], d[0]), sub(b[1], d[1])), 1, 4, sign)
            result[k] = (add(ac[0], bd[0]), add(ac[1], bd[1]))
            result[k + half] = (sub(ac[0], bd[0]), sub(ac[1], bd[1]))
            result[k + quarter] = (add(am[0], bm[0]), add(am[1], bm[1]))
            result[k + half + quarter] = (sub(am[0], bm[0]), sub(am[1], bm[1]))
        return result
    even = complex_dft(values[0::2], sign)
    odd = complex_dft(values[1::2], sign)
    result = [None] * count
    for k in range(half):
        o = turn(odd[k], k, count, sign)
        result[k] = (add(even[k][0], o[0]), add(even[k][1], o[1]))
        result[k + half] = (sub(even[k][0], o[0]), sub(even[k][1], o[1]))
    return result


def odd_outputs(diff, total, emit, stride):
    quarter = total // 4
    turned = [turn((diff[n], neg(diff[n + quarter])), n, total, -1) for n in range(quarter)]
    for p, (re, im) in enumerate(complex_dft(turned, -1)):
        k = 4 * p + 1
        if k <= total // 2:
            emit(k * stride, re, im)
        else:
            emit((total - k) * stride, re, neg(im))


def real_dft(x, emit, stride):
    total = len(x)
    if total == 1:
        emit(0, x[0], None)
        return
    if total == 2:
        emit(0, x[0] + x[1], None)
        emit(stride, x[0] - x[1], None)
        return
    half = total // 2
    odd_outputs([x[n] - x[n + half] for n in range(half)], total, emit, stride)
    real_dft([x[n] + x[n + half] for n in range(half)], emit, 2 * stride)


def padded_real_dft(load, count, emit):
    odd_outputs([load(n) for n in range(count)], 2 * count, emit, 1)
    real_dft([load(n) for n in range(count)], emit, 2)


def real_inverse(fetch, total, stride, count):
    if total == 2:
        low, high = fetch(0)[0], fetch(stride)[0]
        return [low + high, low - high][:count]
    quarter, half = total // 4, total // 2
    spectrum = []
    for p in range(quarter):
        k = 4 * p + 1
        if k <= half:
            spectrum.append(fetch(k * stride))
        else:
            re, im = fetch((total - k) * stride)
            spectrum.append((re, neg(im)))
    h = [turn(v, n, total, 1) for n, v in enumerate(complex_dft(spectrum, 1))]
    odd = [re for re, im in h] + [neg(im) for re, im in h]
    even = real_inverse(fetch, half, 2 * stride, half)
    result = [even[n] + odd[n] for n in range(half)]
    if count > half:
        result += [even[n] - odd[n] for n in range(half)]
    return result


def tables(blocks):
    k = np.arange(LANES)
    angle = 2.0 * np.pi * (np.outer(k, k) % LANES) / LANES
    cos, sin = np.cos(angle), np.sin(angle)
    forward = np.block([[cos, -sin], [sin, cos]])
    inverse = np.block([[cos, sin], [-sin, cos]]) / (blocks * LANES)
    phase = 2.0 * np.pi * np.outer(np.arange(blocks + 1), k) / (2 * blocks * LANES)
    spread = lambda t: np.ascontiguousarray(
        np.broadcast_to(t[:, None, :], (blocks + 1, 8, LANES)).astype(np.float32)
    )
    return (
        forward.astype(ml_dtypes.bfloat16),
        inverse.astype(ml_dtypes.bfloat16),
        spread(np.cos(phase)),
        spread(np.sin(phase)),
    )


def kernel(
    blocks, dps,
    tok_in, emb_in, taps_in, fil_in, skip_in, cot_in, wf_in, wi_in, tc_in, ts_in,
    out_ref, gfil_ref, gskip_ref, gtaps_ref,
    tok, cot, fil, emb, taps, wf, wi, tc, ts,
    emb_t, tapb, skb, lag, stream, gat, bak, work, fspec, gspec, inv, inv2, conv, resp, outb,
    rs_out, rs_in, tp_out, tp_in, tg_out, tg_in,
    load_sem, own_sem, tok_send, tok_recv, cot_send, cot_recv, out_send, out_recv,
    rs_send, rs_recv, tp_send, tp_recv, tg_send, tg_recv,
):
    S, DP = blocks, dps
    C = fil.shape[0]
    K1 = S + 1
    V = emb.shape[0]
    me = lax.axis_index("seq")
    mine = lax.axis_index("dp")
    window = (me * C) // LANES
    offset = (me * C) % LANES

    def peer_of(k):
        line = min(8, S)
        step = k % line
        odd = step % 2
        dz = odd * ((step + 1) // 2) + (1 - odd) * ((line - step // 2) % line)
        return ((me // line + k // line) % (S // line)) * line + (me + dz) % line

    barrier = pltpu.get_barrier_semaphore()

    @pl.loop(1, S)
    def _(k):
        pl.semaphore_signal(barrier, inc=1, device_id={"seq": (me + k) % S}, device_id_type=MESH)

    @pl.loop(1, DP)
    def _(k):
        pl.semaphore_signal(barrier, inc=1, device_id={"dp": (mine + k) % DP}, device_id_type=MESH)

    lane_start = pl.multiple_of(window * LANES, LANES)
    loads = [
        (fil_in, fil),
        (wf_in, wf),
        (tc_in, tc),
        (ts_in, ts),
        (emb_in.at[:, pl.ds(lane_start, LANES)], emb),
        (taps_in.at[:, :, pl.ds(lane_start, LANES)], taps),
        (wi_in, wi),
        (tok_in, tok.at[me]),
        (cot_in.at[0, pl.ds(pl.multiple_of(me * C, C), C)], cot.at[me]),
    ]
    loads = [pltpu.make_async_copy(a, b, load_sem.at[i]) for i, (a, b) in enumerate(loads)]
    for copy in loads:
        copy.start()

    pl.semaphore_wait(barrier, S - 1 + DP - 1)

    def tok_copy(k, slot):
        return pltpu.make_async_remote_copy(
            src_ref=tok_in, dst_ref=tok.at[slot], send_sem=tok_send.at[k], recv_sem=tok_recv.at[slot],
            device_id={"seq": peer_of(k)}, device_id_type=MESH)

    def cot_copy(k, slot):
        return pltpu.make_async_remote_copy(
            src_ref=cot_in.at[0, pl.ds(pl.multiple_of(peer_of(k) * C, C), C)],
            dst_ref=cot.at[slot], send_sem=cot_send.at[k], recv_sem=cot_recv.at[slot],
            device_id={"seq": peer_of(k)}, device_id_type=MESH)

    def out_copy(k, slot):
        return pltpu.make_async_remote_copy(
            src_ref=outb.at[peer_of(k)], dst_ref=out_ref.at[0, pl.ds(pl.multiple_of(slot * C, C), C)],
            send_sem=out_send.at[k], recv_sem=out_recv.at[slot],
            device_id={"seq": peer_of(k)}, device_id_type=MESH)

    def rs_copy(target, slot):
        return pltpu.make_async_remote_copy(
            src_ref=rs_out.at[target], dst_ref=rs_in.at[slot],
            send_sem=rs_send.at[target], recv_sem=rs_recv.at[slot],
            device_id={"dp": target}, device_id_type=MESH)

    def tp_copy(k, slot):
        return pltpu.make_async_remote_copy(
            src_ref=tp_out, dst_ref=tp_in.at[slot], send_sem=tp_send.at[k], recv_sem=tp_recv.at[slot],
            device_id={"dp": (mine + k) % DP}, device_id_type=MESH)

    def tg_copy(k, slot):
        return pltpu.make_async_remote_copy(
            src_ref=tg_out, dst_ref=tg_in.at[slot], send_sem=tg_send.at[k], recv_sem=tg_recv.at[slot],
            device_id={"seq": peer_of(k)}, device_id_type=MESH)

    @pl.loop(1, S)
    def _(k):
        tok_copy(k, me).start()

    @pl.loop(1, S)
    def _(k):
        cot_copy(k, me).start()

    def spread_stage(load_block):
        @pl.loop(0, C // 8)
        def _(group):
            rows = pl.ds(pl.multiple_of(group * 8, 8), 8)

            def emit(k1, re, im):
                if k1 == 0:
                    work[k1, rows, :LANES] = re
                    work[k1, rows, LANES:] = jnp.zeros_like(re)
                    return
                cos, sin = tc[k1], ts[k1]
                if im is None:
                    work[k1, rows, :LANES] = re * cos
                    work[k1, rows, LANES:] = -(re * sin)
                    return
                work[k1, rows, :LANES] = re * cos + im * sin
                work[k1, rows, LANES:] = im * cos - re * sin

            padded_real_dft(lambda n: load_block(n, rows), S, emit)

    def gather_stage(source, store):
        @pl.loop(0, C // 8)
        def _(group):
            rows = pl.ds(pl.multiple_of(group * 8, 8), 8)

            def fetch(k1):
                if k1 == 0:
                    return (source[k1, rows, :LANES] * 0.5, None)
                re, im = source[k1, rows, :LANES], source[k1, rows, LANES:]
                cos, sin = tc[k1], ts[k1]
                if k1 == S:
                    return ((re * cos - im * sin) * 0.5, None)
                return (re * cos - im * sin, im * cos + re * sin)

            store(group, rows, real_inverse(fetch, 2 * S, 1, S))

    chunk = 11 if K1 % 11 == 0 else 3

    def matrix(value, table):
        flat = value.reshape(chunk * C, 2 * LANES).astype(BF16)
        result = jnp.dot(flat, table[...], preferred_element_type=F32)
        return result.reshape(chunk, C, 2 * LANES)

    def halves(value):
        return value[..., :LANES], value[..., LANES:]

    def joined(re, im):
        return jnp.concatenate([re, im], axis=-1)

    for i in (0, 1, 2, 3):
        loads[i].wait()
    spread_stage(lambda n, rows: fil[rows, n * LANES : (n + 1) * LANES])

    @pl.loop(0, K1 // chunk)
    def _(i):
        part = pl.ds(i * chunk, chunk)
        fspec[part] = matrix(work[part], wf)

    for i in (4, 5, 6, 7, 8):
        loads[i].wait()
    lane_id = lax.broadcasted_iota(jnp.int32, (C, LANES), 1)
    own_lane = lane_id == lax.broadcasted_iota(jnp.int32, (C, LANES), 0) + offset

    def column(row):
        picked = jnp.where(own_lane, jnp.broadcast_to(row, (C, LANES)), 0.0)
        return jnp.broadcast_to(jnp.sum(picked, axis=1, keepdims=True), (C, LANES))

    for j in range(3):
        for i in range(3):
            tapb[3 * j + i] = column(taps[j, i : i + 1, :])
    skip_row = jnp.broadcast_to(skip_in[...], (C, C))
    diagonal = lax.broadcasted_iota(jnp.int32, (C, C), 0) == lax.broadcasted_iota(jnp.int32, (C, C), 1)
    skb[...] = jnp.broadcast_to(
        jnp.sum(jnp.where(diagonal, skip_row, 0.0), axis=1, keepdims=True), (C, LANES))
    emb_t[...] = lax.dot_general(
        jnp.where(own_lane, 1.0, 0.0).astype(BF16), emb[...], (((1,), (1,)), ((), ())),
        preferred_element_type=F32).astype(BF16)

    @pl.loop(1, S)
    def _(k):
        tok_copy(k, peer_of(k)).wait_recv()

    vocab_id = lax.broadcasted_iota(jnp.int32, (V, 2 * LANES), 0)

    def stream_pair(m, carry):
        row = jnp.concatenate([tok[2 * m], tok[2 * m + 1]], axis=1)
        onehot = jnp.where(vocab_id == row, 1.0, 0.0).astype(BF16)
        pair = jnp.dot(emb_t[...], onehot, preferred_element_type=F32)
        before1, before2 = carry
        for part in range(2):
            n = 2 * m + part
            lag0 = pair[:, part * LANES : (part + 1) * LANES]
            turned1, turned2 = pltpu.roll(lag0, 1, 1), pltpu.roll(lag0, 2, 1)
            lag1 = jnp.where(lane_id < 1, before1, turned1)
            lag2 = jnp.where(lane_id < 2, before2, turned2)
            before1, before2 = turned1, turned2
            for i, value in enumerate((lag0, lag1, lag2)):
                lag[i, n] = value.astype(BF16)
            streams = []
            for j in range(3):
                total = tapb[3 * j] * lag0 + tapb[3 * j + 1] * lag1 + tapb[3 * j + 2] * lag2
                rounded = total.astype(BF16)
                stream[j, n] = rounded
                streams.append(rounded.astype(F32))
            gat[n] = (streams[0] * streams[2]).astype(BF16).astype(F32)
        return (before1, before2)

    zero = jnp.zeros((C, LANES), F32)
    lax.fori_loop(0, S // 2, stream_pair, (zero, zero))

    spread_stage(lambda n, rows: gat[n, rows])

    @pl.loop(0, K1 // chunk)
    def _(i):
        part = pl.ds(i * chunk, chunk)
        spectrum = matrix(work[part], wf)
        gspec[part] = spectrum
        gr, gi = halves(spectrum)
        fr, fi = halves(fspec[part])
        inv[part] = matrix(joined(gr * fr - gi * fi, gr * fi + gi * fr), wi)

    def keep(group, rows, values):
        for n, value in enumerate(values):
            conv[n, rows] = value

    gather_stage(inv, keep)

    @pl.loop(0, S)
    def _(k):
        n = peer_of(k)
        response = (conv[n] + skb[...] * gat[n]).astype(BF16)
        resp[n] = response
        outb[n] = (stream[1, n].astype(F32) * response.astype(F32)).astype(BF16)

        @pl.when(k > 0)
        def _():
            out_copy(k, me).start()

    own_out = pltpu.make_async_copy(
        outb.at[me], out_ref.at[0, pl.ds(pl.multiple_of(me * C, C), C)], own_sem)
    own_out.start()

    @pl.loop(1, S)
    def _(k):
        cot_copy(k, peer_of(k)).wait_recv()

    sums = [[] for _ in range(10)]
    for part in range(C // 16):
        rows = pl.ds(part * 16, 16)

        def back_block(n, carry):
            cot_f = cot[n, rows].astype(F32)
            back = (cot_f * stream[1, n, rows].astype(F32)).astype(BF16).astype(F32)
            bak[n, rows] = back
            grad = cot_f * resp[n, rows].astype(F32)
            fresh = [grad * lag[i, n, rows].astype(F32) for i in range(3)] + [back * gat[n, rows]]
            return tuple(a + b for a, b in zip(carry, fresh))

        start = jnp.zeros((16, LANES), F32)
        found = lax.fori_loop(0, S, back_block, (start,) * 4)
        for j, value in zip((3, 4, 5, 9), found):
            sums[j].append(value)

    spread_stage(lambda n, rows: bak[n, rows])

    @pl.loop(0, K1 // chunk)
    def _(i):
        part = pl.ds(i * chunk, chunk)
        br, bi = halves(matrix(work[part], wf))
        gr, gi = halves(gspec[part])
        inv2[part] = matrix(joined(gr * br + gi * bi, gr * bi - gi * br), wi)
        fr, fi = halves(fspec[part])
        inv[part] = matrix(joined(br * fr + bi * fi, bi * fr - br * fi), wi)

    def send_filter(group, rows, values):
        for m in range(S // 2):
            both = jnp.concatenate([values[2 * m], values[2 * m + 1]], axis=0)
            rs_out[group, 16 * m : 16 * m + 16] = both.astype(BF16)

        @pl.when(group != mine)
        def _():
            rs_copy(group, mine).start()

    gather_stage(inv2, send_filter)
    gather_stage(inv, keep)

    for part in range(C // 16):
        rows = pl.ds(part * 16, 16)
        skip_part = skb[rows]

        def grad_block(n, carry):
            grad = (conv[n, rows] + skip_part * bak[n, rows]).astype(BF16).astype(F32)
            grad_first = grad * stream[2, n, rows].astype(F32)
            grad_value = grad * stream[0, n, rows].astype(F32)
            lags = [lag[i, n, rows].astype(F32) for i in range(3)]
            fresh = [grad_first * one for one in lags] + [grad_value * one for one in lags]
            return tuple(a + b for a, b in zip(carry, fresh))

        start = jnp.zeros((16, LANES), F32)
        found = lax.fori_loop(0, S, grad_block, (start,) * 6)
        for j, value in zip((0, 1, 2, 6, 7, 8), found):
            sums[j].append(value)

    tp_out[...] = jnp.zeros_like(tp_out)
    for j in range(10):
        total = jnp.sum(jnp.concatenate(sums[j], axis=0), axis=1, keepdims=True)
        placed = jnp.where(own_lane, jnp.broadcast_to(total, (C, LANES)), 0.0)
        tp_out[j : j + 1, :] = jnp.sum(placed, axis=0, keepdims=True)

    @pl.loop(1, DP)
    def _(k):
        tp_copy(k, mine).start()

    tp_in[mine] = tp_out[...]

    @pl.loop(1, DP)
    def _(k):
        tp_copy(k, (mine + k) % DP).wait_recv()

    total = tp_in[0]
    for i in range(1, DP):
        total = total + tp_in[i]
    tg_out[...] = total

    @pl.loop(1, S)
    def _(k):
        tg_copy(k, me).start()

    tg_in[me] = total
    skip_row = pltpu.roll(total, (LANES - offset - 8 * mine) % LANES, 1)
    gskip_ref[...] = skip_row[9:10, :8]

    rs_in[mine] = rs_out[mine]

    @pl.loop(1, DP)
    def _(k):
        rs_copy((mine + k) % DP, (mine + k) % DP).wait_recv()

    for m in range(S // 2):
        both = rs_in[0, 16 * m : 16 * m + 16].astype(F32)
        for i in range(1, DP):
            both = both + rs_in[i, 16 * m : 16 * m + 16].astype(F32)
        gfil_ref[:, 2 * m * LANES : (2 * m + 1) * LANES] = both[:8]
        gfil_ref[:, (2 * m + 1) * LANES : (2 * m + 2) * LANES] = both[8:]

    @pl.loop(1, S)
    def _(k):
        tg_copy(k, peer_of(k)).wait_recv()

    share = LANES // C
    for w in range(S // share):
        joint = tg_in[share * w]
        for i in range(1, share):
            joint = joint + tg_in[share * w + i]
        for j in range(3):
            gtaps_ref[j, :, w * LANES : (w + 1) * LANES] = joint[3 * j : 3 * j + 3]

    own_out.wait()

    @pl.loop(1, S)
    def _(k):
        out_copy(k, peer_of(k)).wait_recv()

    @pl.loop(1, S)
    def _(k):
        tok_copy(k, me).wait_send()
        cot_copy(k, me).wait_send()
        out_copy(k, me).wait_send()
        tg_copy(k, me).wait_send()

    @pl.loop(1, DP)
    def _(k):
        rs_copy((mine + k) % DP, mine).wait_send()
        tp_copy(k, mine).wait_send()


def shards(blocks, dps, token_ids, embedding, short_taps, long_filter, skip_gain, out_cotangent):
    S, DP = blocks, dps
    C, length = long_filter.shape
    V, D = embedding.shape
    K1 = S + 1
    forward, inverse, twist_cos, twist_sin = (jnp.asarray(t) for t in tables(S))
    any_spec = pl.BlockSpec(memory_space=pl.ANY)
    vmem = pl.BlockSpec(memory_space=pltpu.VMEM)
    tile = (S, C, LANES)
    spectrum = (K1, C, 2 * LANES)
    dma = lambda n: pltpu.SemaphoreType.DMA((n,))
    scratch = [
        pltpu.VMEM((S, 1, LANES), jnp.int32),
        pltpu.VMEM(tile, BF16),
        pltpu.VMEM((C, length), F32),
        pltpu.VMEM((V, LANES), BF16),
        pltpu.VMEM((3, 3, LANES), F32),
        pltpu.VMEM((2 * LANES, 2 * LANES), BF16),
        pltpu.VMEM((2 * LANES, 2 * LANES), BF16),
        pltpu.VMEM((K1, 8, LANES), F32),
        pltpu.VMEM((K1, 8, LANES), F32),
        pltpu.VMEM((C, V), BF16),
        pltpu.VMEM((9, C, LANES), F32),
        pltpu.VMEM((C, LANES), F32),
        pltpu.VMEM((3,) + tile, BF16),
        pltpu.VMEM((3,) + tile, BF16),
        pltpu.VMEM(tile, F32),
        pltpu.VMEM(tile, F32),
        pltpu.VMEM(spectrum, F32),
        pltpu.VMEM(spectrum, F32),
        pltpu.VMEM(spectrum, F32),
        pltpu.VMEM(spectrum, F32),
        pltpu.VMEM(spectrum, F32),
        pltpu.VMEM(tile, F32),
        pltpu.VMEM(tile, BF16),
        pltpu.VMEM(tile, BF16),
        pltpu.VMEM((DP, S * 8, LANES), BF16),
        pltpu.VMEM((DP, S * 8, LANES), BF16),
        pltpu.VMEM((16, LANES), F32),
        pltpu.VMEM((DP, 16, LANES), F32),
        pltpu.VMEM((16, LANES), F32),
        pltpu.VMEM((S, 16, LANES), F32),
        dma(9),
        pltpu.SemaphoreType.DMA,
        dma(S), dma(S), dma(S), dma(S), dma(S), dma(S),
        dma(DP), dma(DP), dma(DP), dma(DP), dma(S), dma(S),
    ]
    out, grad_filter, grad_skip, grad_taps = pl.pallas_call(
        functools.partial(kernel, S, DP),
        out_shape=(
            jax.ShapeDtypeStruct((1, D, LANES), BF16),
            jax.ShapeDtypeStruct((8, length), F32),
            jax.ShapeDtypeStruct((1, 8), F32),
            jax.ShapeDtypeStruct((3, 3, D), F32),
        ),
        in_specs=[any_spec] * 4 + [vmem] + [any_spec] * 5,
        out_specs=(any_spec, vmem, vmem, vmem),
        scratch_shapes=scratch,
        compiler_params=pltpu.CompilerParams(
            collective_id=0, has_side_effects=True, vmem_limit_bytes=56 * 1024 * 1024
        ),
        cost_estimate=pl.CostEstimate(
            flops=7 * 2 * K1 * C * 256 * 256, bytes_accessed=6 * 1024 * 1024, transcendentals=0
        ),
    )(token_ids, embedding, short_taps, long_filter, skip_gain.reshape(1, C), out_cotangent,
      forward, inverse, twist_cos, twist_sin)
    return (out, grad_filter, grad_skip.reshape(8), grad_taps)


def solution(mesh):
    return jax.shard_map(
        functools.partial(shards, mesh.shape["seq"], mesh.shape["dp"]),
        mesh=mesh,
        in_specs=(P("dp", "seq"), P(), P(), P("seq", None), P("seq"), P("dp", None, "seq")),
        out_specs=(P("dp", None, "seq"), P(("seq", "dp"), None), P(("seq", "dp")), P()),
        check_vma=False,
    )
```

time: 404 us -> 61.9 us (0.15)
  waiting for transfers between devices: 241 us -> 0 us
  Pallas kernels: 0 us -> 55 us
  starting transfers between devices: 39.9 us -> 0 us
  matrix products: 35.7 us -> 0 us
  other arithmetic: 30 us -> 0 us
  blocking collectives: 19 us -> 0 us
  between operations: 16.4 us -> 0.64 us
  local copies, waits for them, and re-layouts: 21 us -> 6.07 us
    psum x1 -> x0, waiting for transfers between devices: 215 us -> none  [shards(): grad_taps = lax.psum(tap_local, ('seq', 'dp'))]
    pallas_call x0 -> x1, Pallas kernels: none -> 55 us  [shards(): pl.pallas_call(functools.partial(kernel, S, DP), out_shape=(jax.ShapeDtyp...]
    dot_general x13 -> x0, matrix products: 35.7 us -> none  [the longest x12 34.5 us: contract(): return jnp.einsum(form, left, right, precision=lax.Precision.HIGH)]
    all_to_all x4 -> x0, starting transfers between devices: 35.4 us -> none  [the longest x1 12.3 us: shards(): lax.all_to_all(shaped[1], 'seq', split_axis=0, concat_axis=2, tiled=True)[0]]
    all_to_all x4 -> x0, waiting for transfers between devices: 26.1 us -> none  [the longest x1 9.28 us: shards(): lax.all_to_all(shaped[1], 'seq', split_axis=0, concat_axis=2, tiled=True)[0]]
    unnamed x1 -> x0, blocking collectives: 19 us -> none
    add x3 -> x0, other arithmetic: 12.7 us -> none  [the longest x1 6.19 us: spectral(): back_re * filter_re + back_im * filter_im]
    convert_element_type x6 -> x0, local copies, waits for them, and re-layouts: 9.27 us -> none  [the longest x1 2.58 us: shards(): response_f = returned[0].reshape(width, local_len).astype(jnp.float32)]
  transfers between devices with their start and end apart: 7 -> 0, of which waited for: 6 -> 0; matrix products, arithmetic and copies ran while one was open for 8% -> 0% of each run, Pallas kernels for 0% -> 0%
where the time goes in v1:
time: 61.9 us; the launch traced here: 61.7 us
  Pallas kernels  55 us (89%)
  local copies, waits for them, and re-layouts  6.07 us (10%)
  between operations  0.64 us (1%)
    pallas_call x1, Pallas kernels, shards(): pl.pallas_call(functools.partial(kernel, S, DP), out_shape=(jax.ShapeDtyp...  55 us
    unnamed x4, local copies, waits for them, and re-layouts  6.07 us

profile of v1, /device:TPU:1, one launch (start us, length us, event | category | flops | bytes accessed | tf_op | source)
XLA Modules:
  0.0 61.7 jit_solution(5604160705235230567)
XLA Ops:
  0.6 55.0 %shard_map.129 = (bf16[1,2048,128]{2,1,0:T(8,128)(2,1)}, f32[8,4096]{1,0:T(8,128)}, f32[1,8]{1,0:T(1,128)}, f32[3,3,2048]{2,1,0:T(4,128)}) custom-call(s32[1,128]{1,0:T(1,128)} %tok_in.1, bf16[512,2048]{1,0:T(8,128)(2,1)} %emb_in.1, f32[3,3,2048]{2,1,0:T(4,128)} %taps_in.1, f32[64,4096]{1,0:T(8,128)} %fil_in.1, f32[1,64]{1,0:T(1,128)} %bitcast.2, ...), custom_call_target="tpu_custom_call" | custom-call | flops 1937768448 | bytes 6291456 | tf_op jit(solution)/shard_map/pallas_call | solution.py:583
  55.7 1.9 %copy.18 = bf16[1,2048,128]{2,1,0:T(8,128)(2,1)} copy(bf16[1,2048,128]{2,1,0:T(8,128)(2,1)} %get-tuple-element.16) | data formatting | bytes 1048576
  57.5 1.6 %copy.19 = f32[8,4096]{1,0:T(8,128)} copy(f32[8,4096]{1,0:T(8,128)} %get-tuple-element.17) | data formatting | bytes 262144
  59.1 1.1 %copy.20 = f32[8]{0:T(128)} copy(f32[8]{0:T(128)} %bitcast.3) | data formatting | bytes 64
  60.2 1.5 %copy.21 = f32[3,3,2048]{2,1,0:T(4,128)} copy(f32[3,3,2048]{2,1,0:T(4,128)} %get-tuple-element.19) | data formatting | bytes 147456

commit v2 on v1

--- a/solution.py
+++ b/solution.py
@@ -167,7 +167,7 @@
     tok_in, emb_in, taps_in, fil_in, skip_in, cot_in, wf_in, wi_in, tc_in, ts_in,
     out_ref, gfil_ref, gskip_ref, gtaps_ref,
     tok, cot, fil, emb, taps, wf, wi, tc, ts,
-    emb_t, tapb, skb, lag, stream, gat, bak, work, fspec, gspec, inv, inv2, conv, resp, outb,
+    emb_t, tapb, skb, lag, stream, gat, bak, work, fspec, gspec, bspec, inv, conv, resp, outb,
     rs_out, rs_in, tp_out, tp_in, tg_out, tg_in,
     load_sem, own_sem, tok_send, tok_recv, cot_send, cot_recv, out_send, out_recv,
     rs_send, rs_recv, tp_send, tp_recv, tg_send, tg_recv,
@@ -181,22 +181,32 @@
     window = (me * C) // LANES
     offset = (me * C) % LANES
 
-    def peer_of(k):
-        line = min(8, S)
-        step = k % line
-        odd = step % 2
-        dz = odd * ((step + 1) // 2) + (1 - odd) * ((line - step // 2) % line)
-        return ((me // line + k // line) % (S // line)) * line + (me + dz) % line
+    line = min(8, S)
+    planes = S // line
+    me_x, me_z = me // line, me % line
+
+    def wrapped(value, size):
+        return jnp.where(value >= size, value - size, value)
+
+    def peer_at(step):
+        return wrapped(me_x + step[0], planes) * line + wrapped(me_z + step[1], line)
+
+    def around(k):
+        there = me + k
+        return jnp.where(there < 0, there + S, wrapped(there, S))
+
+    def dp_at(k):
+        return wrapped(mine + k, DP)
+
+    turns = [(i + 1) // 2 if i % 2 else (line - i // 2) % line for i in range(line)]
+    steps = [(dx, dz) for dz in turns for dx in range(planes)][1:]
 
     barrier = pltpu.get_barrier_semaphore()
 
-    @pl.loop(1, S)
-    def _(k):
-        pl.semaphore_signal(barrier, inc=1, device_id={"seq": (me + k) % S}, device_id_type=MESH)
-
-    @pl.loop(1, DP)
-    def _(k):
-        pl.semaphore_signal(barrier, inc=1, device_id={"dp": (mine + k) % DP}, device_id_type=MESH)
+    for step in steps:
+        pl.semaphore_signal(barrier, inc=1, device_id={"seq": peer_at(step)}, device_id_type=MESH)
+    for k in range(1, DP):
+        pl.semaphore_signal(barrier, inc=1, device_id={"dp": dp_at(k)}, device_id_type=MESH)
 
     lane_start = pl.multiple_of(window * LANES, LANES)
     loads = [
@@ -216,46 +226,47 @@
 
     pl.semaphore_wait(barrier, S - 1 + DP - 1)
 
-    def tok_copy(k, slot):
+    def tok_copy(peer):
         return pltpu.make_async_remote_copy(
-            src_ref=tok_in, dst_ref=tok.at[slot], send_sem=tok_send.at[k], recv_sem=tok_recv.at[slot],
-            device_id={"seq": peer_of(k)}, device_id_type=MESH)
-
-    def cot_copy(k, slot):
+            src_ref=tok_in, dst_ref=tok.at[me], send_sem=tok_send, recv_sem=tok_recv,
+            device_id={"seq": peer}, device_id_type=MESH)
+
+    def cot_copy(peer):
         return pltpu.make_async_remote_copy(
-            src_ref=cot_in.at[0, pl.ds(pl.multiple_of(peer_of(k) * C, C), C)],
-            dst_ref=cot.at[slot], send_sem=cot_send.at[k], recv_sem=cot_recv.at[slot],
-            device_id={"seq": peer_of(k)}, device_id_type=MESH)
-
-    def out_copy(k, slot):
+            src_ref=cot_in.at[0, pl.ds(pl.multiple_of(peer * C, C), C)],
+            dst_ref=cot.at[me], send_sem=cot_send, recv_sem=cot_recv,
+            device_id={"seq": peer}, device_id_type=MESH)
+
+    def out_copy(peer):
         return pltpu.make_async_remote_copy(
-            src_ref=outb.at[peer_of(k)], dst_ref=out_ref.at[0, pl.ds(pl.multiple_of(slot * C, C), C)],
-            send_sem=out_send.at[k], recv_sem=out_recv.at[slot],
-            device_id={"seq": peer_of(k)}, device_id_type=MESH)
-
-    def rs_copy(target, slot):
+            src_ref=outb.at[peer], dst_ref=out_ref.at[0, pl.ds(pl.multiple_of(me * C, C), C)],
+            send_sem=out_send, recv_sem=out_recv,
+            device_id={"seq": peer}, device_id_type=MESH)
+
+    def rs_copy(target):
         return pltpu.make_async_remote_copy(
-            src_ref=rs_out.at[target], dst_ref=rs_in.at[slot],
-            send_sem=rs_send.at[target], recv_sem=rs_recv.at[slot],
+            src_ref=rs_out.at[target], dst_ref=rs_in.at[mine],
+            send_sem=rs_send, recv_sem=rs_recv,
             device_id={"dp": target}, device_id_type=MESH)
 
-    def tp_copy(k, slot):
+    def tp_copy(target):
         return pltpu.make_async_remote_copy(
-            src_ref=tp_out, dst_ref=tp_in.at[slot], send_sem=tp_send.at[k], recv_sem=tp_recv.at[slot],
-            device_id={"dp": (mine + k) % DP}, device_id_type=MESH)
-
-    def tg_copy(k, slot):
+            src_ref=tp_out, dst_ref=tp_in.at[mine], send_sem=tp_send, recv_sem=tp_recv,
+            device_id={"dp": target}, device_id_type=MESH)
+
+    def tg_copy(peer):
         return pltpu.make_async_remote_copy(
-            src_ref=tg_out, dst_ref=tg_in.at[slot], send_sem=tg_send.at[k], recv_sem=tg_recv.at[slot],
-            device_id={"seq": peer_of(k)}, device_id_type=MESH)
-
-    @pl.loop(1, S)
-    def _(k):
-        tok_copy(k, me).start()
-
-    @pl.loop(1, S)
-    def _(k):
-        cot_copy(k, me).start()
+            src_ref=tg_out, dst_ref=tg_in.at[me], send_sem=tg_send, recv_sem=tg_recv,
+            device_id={"seq": peer}, device_id_type=MESH)
+
+    def wait_all(buffer, count, sem):
+        part = buffer.at[pl.ds(0, count)]
+        pltpu.make_async_copy(part, part, sem).wait()
+
+    for step in steps:
+        tok_copy(peer_at(step)).start()
+    for step in steps:
+        cot_copy(peer_at(step)).start()
 
     def spread_stage(load_block):
         @pl.loop(0, C // 8)
@@ -335,9 +346,7 @@
         jnp.where(own_lane, 1.0, 0.0).astype(BF16), emb[...], (((1,), (1,)), ((), ())),
         preferred_element_type=F32).astype(BF16)
 
-    @pl.loop(1, S)
-    def _(k):
-        tok_copy(k, peer_of(k)).wait_recv()
+    wait_all(tok, S - 1, tok_recv)
 
     vocab_id = lax.broadcasted_iota(jnp.int32, (V, 2 * LANES), 0)
 
@@ -384,24 +393,28 @@
 
     gather_stage(inv, keep)
 
-    @pl.loop(0, S)
-    def _(k):
-        n = peer_of(k)
+    def finish_block(n):
         response = (conv[n] + skb[...] * gat[n]).astype(BF16)
         resp[n] = response
         outb[n] = (stream[1, n].astype(F32) * response.astype(F32)).astype(BF16)
 
-        @pl.when(k > 0)
-        def _():
-            out_copy(k, me).start()
-
+    @pl.loop(1, S // 2)
+    def _(k):
+        ahead, behind = around(k), around(-k)
+        finish_block(ahead)
+        out_copy(ahead).start()
+        finish_block(behind)
+        out_copy(behind).start()
+
+    opposite = around(S // 2)
+    finish_block(opposite)
+    out_copy(opposite).start()
+    finish_block(me)
     own_out = pltpu.make_async_copy(
         outb.at[me], out_ref.at[0, pl.ds(pl.multiple_of(me * C, C), C)], own_sem)
     own_out.start()
 
-    @pl.loop(1, S)
-    def _(k):
-        cot_copy(k, peer_of(k)).wait_recv()
+    wait_all(cot, S - 1, cot_recv)
 
     sums = [[] for _ in range(10)]
     for part in range(C // 16):
@@ -425,22 +438,12 @@
     @pl.loop(0, K1 // chunk)
     def _(i):
         part = pl.ds(i * chunk, chunk)
-        br, bi = halves(matrix(work[part], wf))
-        gr, gi = halves(gspec[part])
-        inv2[part] = matrix(joined(gr * br + gi * bi, gr * bi - gi * br), wi)
+        spectrum = matrix(work[part], wf)
+        bspec[part] = spectrum
+        br, bi = halves(spectrum)
         fr, fi = halves(fspec[part])
         inv[part] = matrix(joined(br * fr + bi * fi, bi * fr - br * fi), wi)
 
-    def send_filter(group, rows, values):
-        for m in range(S // 2):
-            both = jnp.concatenate([values[2 * m], values[2 * m + 1]], axis=0)
-            rs_out[group, 16 * m : 16 * m + 16] = both.astype(BF16)
-
-        @pl.when(group != mine)
-        def _():
-            rs_copy(group, mine).start()
-
-    gather_stage(inv2, send_filter)
     gather_stage(inv, keep)
 
     for part in range(C // 16):
@@ -460,41 +463,48 @@
         for j, value in zip((0, 1, 2, 6, 7, 8), found):
             sums[j].append(value)
 
-    tp_out[...] = jnp.zeros_like(tp_out)
-    for j in range(10):
+    def placed(j, shift):
         total = jnp.sum(jnp.concatenate(sums[j], axis=0), axis=1, keepdims=True)
-        placed = jnp.where(own_lane, jnp.broadcast_to(total, (C, LANES)), 0.0)
-        tp_out[j : j + 1, :] = jnp.sum(placed, axis=0, keepdims=True)
-
-    @pl.loop(1, DP)
-    def _(k):
-        tp_copy(k, mine).start()
-
+        spot = lane_id == lax.broadcasted_iota(jnp.int32, (C, LANES), 0) + shift
+        kept = jnp.where(spot, jnp.broadcast_to(total, (C, LANES)), 0.0)
+        return jnp.sum(kept, axis=0, keepdims=True)
+
+    tp_out[...] = jnp.concatenate([placed(j, 0) + placed(j + 5, C) for j in range(5)], axis=0)
+    for k in range(1, DP):
+        tp_copy(dp_at(k)).start()
     tp_in[mine] = tp_out[...]
 
-    @pl.loop(1, DP)
-    def _(k):
-        tp_copy(k, (mine + k) % DP).wait_recv()
-
+    @pl.loop(0, K1 // chunk)
+    def _(i):
+        part = pl.ds(i * chunk, chunk)
+        br, bi = halves(bspec[part])
+        gr, gi = halves(gspec[part])
+        inv[part] = matrix(joined(gr * br + gi * bi, gr * bi - gi * br), wi)
+
+    def send_filter(group, rows, values):
+        for m in range(S // 2):
+            both = jnp.concatenate([values[2 * m], values[2 * m + 1]], axis=0)
+            rs_out[group, 16 * m : 16 * m + 16] = both.astype(BF16)
+
+        @pl.when(group != mine)
+        def _():
+            rs_copy(group).start()
+
+    gather_stage(inv, send_filter)
+
+    wait_all(tp_in, DP - 1, tp_recv)
     total = tp_in[0]
     for i in range(1, DP):
         total = total + tp_in[i]
     tg_out[...] = total
-
-    @pl.loop(1, S)
-    def _(k):
-        tg_copy(k, me).start()
-
+    for step in steps:
+        tg_copy(peer_at(step)).start()
     tg_in[me] = total
-    skip_row = pltpu.roll(total, (LANES - offset - 8 * mine) % LANES, 1)
-    gskip_ref[...] = skip_row[9:10, :8]
+    skip_row = pltpu.roll(total, LANES - C - 8 * mine, 1)
+    gskip_ref[...] = skip_row[4:5, :8]
 
     rs_in[mine] = rs_out[mine]
-
-    @pl.loop(1, DP)
-    def _(k):
-        rs_copy((mine + k) % DP, (mine + k) % DP).wait_recv()
-
+    wait_all(rs_in, DP - 1, rs_recv)
     for m in range(S // 2):
         both = rs_in[0, 16 * m : 16 * m + 16].astype(F32)
         for i in range(1, DP):
@@ -502,35 +512,42 @@
         gfil_ref[:, 2 * m * LANES : (2 * m + 1) * LANES] = both[:8]
         gfil_ref[:, (2 * m + 1) * LANES : (2 * m + 2) * LANES] = both[8:]
 
-    @pl.loop(1, S)
-    def _(k):
-        tg_copy(k, peer_of(k)).wait_recv()
-
+    wait_all(tg_in, S - 1, tg_recv)
     share = LANES // C
+    owner = lax.broadcasted_iota(jnp.int32, (5, LANES), 1) // C
+
+    def shift(value, places):
+        return pltpu.roll(value, places % LANES, 1) if places % LANES else value
+
     for w in range(S // share):
-        joint = tg_in[share * w]
-        for i in range(1, share):
-            joint = joint + tg_in[share * w + i]
-        for j in range(3):
-            gtaps_ref[j, :, w * LANES : (w + 1) * LANES] = joint[3 * j : 3 * j + 3]
+        low = high = jnp.zeros((5, LANES), F32)
+        for q in range(share):
+            block = tg_in[share * w + q]
+            low = jnp.where(owner == q, shift(block, q * C), low)
+            high = jnp.where(owner == q, shift(block, (q - 1) * C), high)
+        lanes = slice(w * LANES, (w + 1) * LANES)
+        gtaps_ref[0, :, lanes] = low[0:3]
+        gtaps_ref[1, 0:2, lanes] = low[3:5]
+        gtaps_ref[1, 2:3, lanes] = high[0:1]
+        gtaps_ref[2, :, lanes] = high[1:4]
 
     own_out.wait()
-
-    @pl.loop(1, S)
-    def _(k):
-        out_copy(k, peer_of(k)).wait_recv()
-
-    @pl.loop(1, S)
-    def _(k):
-        tok_copy(k, me).wait_send()
-        cot_copy(k, me).wait_send()
-        out_copy(k, me).wait_send()
-        tg_copy(k, me).wait_send()
-
-    @pl.loop(1, DP)
-    def _(k):
-        rs_copy((mine + k) % DP, mine).wait_send()
-        tp_copy(k, mine).wait_send()
+    wait_all(outb, S - 1, out_recv)
+    wait_all(tok, S - 1, tok_send)
+    wait_all(cot, S - 1, cot_send)
+    wait_all(outb, S - 1, out_send)
+    wait_all(tg_in, S - 1, tg_send)
+    wait_all(rs_in, DP - 1, rs_send)
+    wait_all(tp_in, DP - 1, tp_send)
+
+
+def hand_over(*refs):
+    sources, results, sems = refs[:4], refs[4:8], refs[8]
+    copies = [pltpu.make_async_copy(a, b, sems.at[i]) for i, (a, b) in enumerate(zip(sources, results))]
+    for copy in copies:
+        copy.start()
+    for copy in copies:
+        copy.wait()
 
 
 def shards(blocks, dps, token_ids, embedding, short_taps, long_filter, skip_gain, out_cotangent):
@@ -571,23 +588,21 @@
         pltpu.VMEM(tile, BF16),
         pltpu.VMEM((DP, S * 8, LANES), BF16),
         pltpu.VMEM((DP, S * 8, LANES), BF16),
-        pltpu.VMEM((16, LANES), F32),
-        pltpu.VMEM((DP, 16, LANES), F32),
-        pltpu.VMEM((16, LANES), F32),
-        pltpu.VMEM((S, 16, LANES), F32),
+        pltpu.VMEM((5, LANES), F32),
+        pltpu.VMEM((DP, 5, LANES), F32),
+        pltpu.VMEM((5, LANES), F32),
+        pltpu.VMEM((S, 5, LANES), F32),
         dma(9),
-        pltpu.SemaphoreType.DMA,
-        dma(S), dma(S), dma(S), dma(S), dma(S), dma(S),
-        dma(DP), dma(DP), dma(DP), dma(DP), dma(S), dma(S),
-    ]
-    out, grad_filter, grad_skip, grad_taps = pl.pallas_call(
+    ] + [pltpu.SemaphoreType.DMA] * 13
+    shapes = (
+        jax.ShapeDtypeStruct((1, D, LANES), BF16),
+        jax.ShapeDtypeStruct((8, length), F32),
+        jax.ShapeDtypeStruct((1, 8), F32),
+        jax.ShapeDtypeStruct((3, 3, D), F32),
+    )
+    results = pl.pallas_call(
         functools.partial(kernel, S, DP),
-        out_shape=(
-            jax.ShapeDtypeStruct((1, D, LANES), BF16),
-            jax.ShapeDtypeStruct((8, length), F32),
-            jax.ShapeDtypeStruct((1, 8), F32),
-            jax.ShapeDtypeStruct((3, 3, D), F32),
-        ),
+        out_shape=shapes,
         in_specs=[any_spec] * 4 + [vmem] + [any_spec] * 5,
         out_specs=(any_spec, vmem, vmem, vmem),
         scratch_shapes=scratch,
@@ -599,6 +614,13 @@
         ),
     )(token_ids, embedding, short_taps, long_filter, skip_gain.reshape(1, C), out_cotangent,
       forward, inverse, twist_cos, twist_sin)
+    out, grad_filter, grad_skip, grad_taps = pl.pallas_call(
+        hand_over,
+        out_shape=shapes,
+        in_specs=[any_spec] * 4,
+        out_specs=(any_spec,) * 4,
+        scratch_shapes=[dma(4)],
+    )(*results)
     return (out, grad_filter, grad_skip.reshape(8), grad_taps)
 
 

time: 61.9 us -> 71.9 us (1.16)
  Pallas kernels: 55 us -> 71.2 us
  local copies, waits for them, and re-layouts: 6.07 us -> 0 us
    pallas_call x1 -> x2, Pallas kernels: 55 us -> 71.2 us  [the longest x1 47.2 us: shards(): pl.pallas_call(functools.partial(kernel, S, DP), out_shape=shapes, in_spe...]
    unnamed x4 -> x0, local copies, waits for them, and re-layouts: 6.07 us -> none
where the time goes in v2:
time: 71.9 us; the launch traced here: 71.8 us
  Pallas kernels  71.2 us (99%)
    pallas_call x1, Pallas kernels, shards(): pl.pallas_call(functools.partial(kernel, S, DP), out_shape=shapes, in_spe...  47.2 us
    pallas_call x1, Pallas kernels, shards(): pl.pallas_call(hand_over, out_shape=shapes, in_specs=[any_spec] * 4, out_...  24 us

profile of v2, /device:TPU:1, one launch (start us, length us, event | category | flops | bytes accessed | tf_op | source)
XLA Modules:
  0.0 71.8 jit_solution(7797610855381655715)
XLA Ops:
  0.6 47.2 %shard_map.129 = (bf16[1,2048,128]{2,1,0:T(8,128)(2,1)}, f32[8,4096]{1,0:T(8,128)}, f32[1,8]{1,0:T(1,128)}, f32[3,3,2048]{2,1,0:T(4,128)}) custom-call(s32[1,128]{1,0:T(1,128)} %tok_in.1, bf16[512,2048]{1,0:T(8,128)(2,1)} %emb_in.1, f32[3,3,2048]{2,1,0:T(4,128)} %taps_in.1, f32[64,4096]{1,0:T(8,128)} %fil_in.1, f32[1,64]{1,0:T(1,128)} %bitcast.2, ...), custom_call_target="tpu_custom_call" | custom-call | flops 1937768448 | bytes 6291456 | tf_op jit(solution)/shard_map/pallas_call | solution.py:603
  47.9 24.0 %shard_map.130 = (bf16[1,2048,128]{2,1,0:T(8,128)(2,1)}, f32[8,4096]{1,0:T(8,128)}, f32[1,8]{1,0:T(1,128)}, f32[3,3,2048]{2,1,0:T(4,128)}) custom-call(bf16[1,2048,128]{2,1,0:T(8,128)(2,1)} %get-tuple-element.12.refs_0_, f32[8,4096]{1,0:T(8,128)} %get-tuple-element.13.refs_1_, f32[1,8]{1,0:T(1,128)} %get-tuple-element.14.refs_2_, ...), custom_call_target="tpu_custom_call" | custom-call | tf_op jit(solution)/shard_map/pallas_call | solution.py:617

commit v3 on v2

--- a/solution.py
+++ b/solution.py
@@ -542,11 +542,15 @@
 
 
 def hand_over(*refs):
-    sources, results, sems = refs[:4], refs[4:8], refs[8]
-    copies = [pltpu.make_async_copy(a, b, sems.at[i]) for i, (a, b) in enumerate(zip(sources, results))]
-    for copy in copies:
+    sources, results, held, sems = refs[:4], refs[4:8], refs[8:12], refs[12]
+    arrive = [pltpu.make_async_copy(a, b, sems.at[i]) for i, (a, b) in enumerate(zip(sources, held))]
+    leave = [pltpu.make_async_copy(a, b, sems.at[i]) for i, (a, b) in enumerate(zip(held, results))]
+    for copy in arrive:
         copy.start()
-    for copy in copies:
+    for first, second in zip(arrive, leave):
+        first.wait()
+        second.start()
+    for copy in leave:
         copy.wait()
 
 
@@ -619,7 +623,7 @@
         out_shape=shapes,
         in_specs=[any_spec] * 4,
         out_specs=(any_spec,) * 4,
-        scratch_shapes=[dma(4)],
+        scratch_shapes=[pltpu.VMEM(r.shape, r.dtype) for r in shapes] + [dma(4)],
     )(*results)
     return (out, grad_filter, grad_skip.reshape(8), grad_taps)
 

time: 71.9 us -> 49.9 us (0.69)
  Pallas kernels: 71.2 us -> 49.1 us
    pallas_call x1, Pallas kernels: 24 us -> 1.94 us  [shards(): pl.pallas_call(hand_over, out_shape=shapes, in_specs=[any_spec] * 4, out_...]
where the time goes in v3:
time: 49.9 us; the launch traced here: 49.8 us
  Pallas kernels  49.1 us (98%)
  between operations  0.64 us (1%)
    pallas_call x1, Pallas kernels, shards(): pl.pallas_call(functools.partial(kernel, S, DP), out_shape=shapes, in_spe...  47.2 us
    pallas_call x1, Pallas kernels, shards(): pl.pallas_call(hand_over, out_shape=shapes, in_specs=[any_spec] * 4, out_...  1.94 us

profile of v3, /device:TPU:1, one launch (start us, length us, event | category | flops | bytes accessed | tf_op | source)
XLA Modules:
  0.0 49.8 jit_solution(72314205552785962)
XLA Ops:
  0.6 47.2 %shard_map.129 = (bf16[1,2048,128]{2,1,0:T(8,128)(2,1)}, f32[8,4096]{1,0:T(8,128)}, f32[1,8]{1,0:T(1,128)}, f32[3,3,2048]{2,1,0:T(4,128)}) custom-call(s32[1,128]{1,0:T(1,128)} %tok_in.1, bf16[512,2048]{1,0:T(8,128)(2,1)} %emb_in.1, f32[3,3,2048]{2,1,0:T(4,128)} %taps_in.1, f32[64,4096]{1,0:T(8,128)} %fil_in.1, f32[1,64]{1,0:T(1,128)} %bitcast.2, ...), custom_call_target="tpu_custom_call" | custom-call | flops 1937768448 | bytes 6291456 | tf_op jit(solution)/shard_map/pallas_call | solution.py:607
  47.9 1.9 %shard_map.130 = (bf16[1,2048,128]{2,1,0:T(8,128)(2,1)}, f32[8,4096]{1,0:T(8,128)}, f32[1,8]{1,0:T(1,128)}, f32[3,3,2048]{2,1,0:T(4,128)}) custom-call(bf16[1,2048,128]{2,1,0:T(8,128)(2,1)} %get-tuple-element.12.refs_0_, f32[8,4096]{1,0:T(8,128)} %get-tuple-element.13.refs_1_, f32[1,8]{1,0:T(1,128)} %get-tuple-element.14.refs_2_, ...), custom_call_target="tpu_custom_call" | custom-call | tf_op jit(solution)/shard_map/pallas_call | solution.py:621

commit v4 on v3

--- a/solution.py
+++ b/solution.py
@@ -168,7 +168,7 @@
     out_ref, gfil_ref, gskip_ref, gtaps_ref,
     tok, cot, fil, emb, taps, wf, wi, tc, ts,
     emb_t, tapb, skb, lag, stream, gat, bak, work, fspec, gspec, bspec, inv, conv, resp, outb,
-    rs_out, rs_in, tp_out, tp_in, tg_out, tg_in,
+    rs_out, rs_in, tp_out, tp_in, tg_out, tg_in, gfil, gskip, gtaps, skip,
     load_sem, own_sem, tok_send, tok_recv, cot_send, cot_recv, out_send, out_recv,
     rs_send, rs_recv, tp_send, tp_recv, tg_send, tg_recv,
 ):
@@ -200,6 +200,7 @@
 
     turns = [(i + 1) // 2 if i % 2 else (line - i // 2) % line for i in range(line)]
     steps = [(dx, dz) for dz in turns for dx in range(planes)][1:]
+    steps.sort(key=lambda step: -min(step[0], planes - step[0]) - min(step[1], line - step[1]))
 
     barrier = pltpu.get_barrier_semaphore()
 
@@ -217,6 +218,7 @@
         (emb_in.at[:, pl.ds(lane_start, LANES)], emb),
         (taps_in.at[:, :, pl.ds(lane_start, LANES)], taps),
         (wi_in, wi),
+        (skip_in, skip),
         (tok_in, tok.at[me]),
         (cot_in.at[0, pl.ds(pl.multiple_of(me * C, C), C)], cot.at[me]),
     ]
@@ -326,7 +328,7 @@
         part = pl.ds(i * chunk, chunk)
         fspec[part] = matrix(work[part], wf)
 
-    for i in (4, 5, 6, 7, 8):
+    for i in (4, 5, 6, 7, 8, 9):
         loads[i].wait()
     lane_id = lax.broadcasted_iota(jnp.int32, (C, LANES), 1)
     own_lane = lane_id == lax.broadcasted_iota(jnp.int32, (C, LANES), 0) + offset
@@ -338,7 +340,7 @@
     for j in range(3):
         for i in range(3):
             tapb[3 * j + i] = column(taps[j, i : i + 1, :])
-    skip_row = jnp.broadcast_to(skip_in[...], (C, C))
+    skip_row = jnp.broadcast_to(skip[...], (C, C))
     diagonal = lax.broadcasted_iota(jnp.int32, (C, C), 0) == lax.broadcasted_iota(jnp.int32, (C, C), 1)
     skb[...] = jnp.broadcast_to(
         jnp.sum(jnp.where(diagonal, skip_row, 0.0), axis=1, keepdims=True), (C, LANES))
@@ -374,7 +376,7 @@
         return (before1, before2)
 
     zero = jnp.zeros((C, LANES), F32)
-    lax.fori_loop(0, S // 2, stream_pair, (zero, zero))
+    lax.fori_loop(0, S // 2, stream_pair, (zero, zero), unroll=4)
 
     spread_stage(lambda n, rows: gat[n, rows])
 
@@ -398,7 +400,7 @@
         resp[n] = response
         outb[n] = (stream[1, n].astype(F32) * response.astype(F32)).astype(BF16)
 
-    @pl.loop(1, S // 2)
+    @pl.loop(1, S // 2, unroll=3)
     def _(k):
         ahead, behind = around(k), around(-k)
         finish_block(ahead)
@@ -429,7 +431,7 @@
             return tuple(a + b for a, b in zip(carry, fresh))
 
         start = jnp.zeros((16, LANES), F32)
-        found = lax.fori_loop(0, S, back_block, (start,) * 4)
+        found = lax.fori_loop(0, S, back_block, (start,) * 4, unroll=16)
         for j, value in zip((3, 4, 5, 9), found):
             sums[j].append(value)
 
@@ -441,6 +443,24 @@
         spectrum = matrix(work[part], wf)
         bspec[part] = spectrum
         br, bi = halves(spectrum)
+        gr, gi = halves(gspec[part])
+        inv[part] = matrix(joined(gr * br + gi * bi, gr * bi - gi * br), wi)
+
+    def send_filter(group, rows, values):
+        for m in range(S // 2):
+            both = jnp.concatenate([values[2 * m], values[2 * m + 1]], axis=0)
+            rs_out[group, 16 * m : 16 * m + 16] = both.astype(BF16)
+
+        @pl.when(group != mine)
+        def _():
+            rs_copy(group).start()
+
+    gather_stage(inv, send_filter)
+
+    @pl.loop(0, K1 // chunk)
+    def _(i):
+        part = pl.ds(i * chunk, chunk)
+        br, bi = halves(bspec[part])
         fr, fi = halves(fspec[part])
         inv[part] = matrix(joined(br * fr + bi * fi, bi * fr - br * fi), wi)
 
@@ -459,7 +479,7 @@
             return tuple(a + b for a, b in zip(carry, fresh))
 
         start = jnp.zeros((16, LANES), F32)
-        found = lax.fori_loop(0, S, grad_block, (start,) * 6)
+        found = lax.fori_loop(0, S, grad_block, (start,) * 6, unroll=16)
         for j, value in zip((0, 1, 2, 6, 7, 8), found):
             sums[j].append(value)
 
@@ -473,24 +493,6 @@
     for k in range(1, DP):
         tp_copy(dp_at(k)).start()
     tp_in[mine] = tp_out[...]
-
-    @pl.loop(0, K1 // chunk)
-    def _(i):
-        part = pl.ds(i * chunk, chunk)
-        br, bi = halves(bspec[part])
-        gr, gi = halves(gspec[part])
-        inv[part] = matrix(joined(gr * br + gi * bi, gr * bi - gi * br), wi)
-
-    def send_filter(group, rows, values):
-        for m in range(S // 2):
-            both = jnp.concatenate([values[2 * m], values[2 * m + 1]], axis=0)
-            rs_out[group, 16 * m : 16 * m + 16] = both.astype(BF16)
-
-        @pl.when(group != mine)
-        def _():
-            rs_copy(group).start()
-
-    gather_stage(inv, send_filter)
 
     wait_all(tp_in, DP - 1, tp_recv)
     total = tp_in[0]
@@ -501,7 +503,7 @@
         tg_copy(peer_at(step)).start()
     tg_in[me] = total
     skip_row = pltpu.roll(total, LANES - C - 8 * mine, 1)
-    gskip_ref[...] = skip_row[4:5, :8]
+    gskip[...] = skip_row[4:5, :8]
 
     rs_in[mine] = rs_out[mine]
     wait_all(rs_in, DP - 1, rs_recv)
@@ -509,8 +511,15 @@
         both = rs_in[0, 16 * m : 16 * m + 16].astype(F32)
         for i in range(1, DP):
             both = both + rs_in[i, 16 * m : 16 * m + 16].astype(F32)
-        gfil_ref[:, 2 * m * LANES : (2 * m + 1) * LANES] = both[:8]
-        gfil_ref[:, (2 * m + 1) * LANES : (2 * m + 2) * LANES] = both[8:]
+        gfil[:, 2 * m * LANES : (2 * m + 1) * LANES] = both[:8]
+        gfil[:, (2 * m + 1) * LANES : (2 * m + 2) * LANES] = both[8:]
+
+    results = [
+        pltpu.make_async_copy(a, b, load_sem.at[i])
+        for i, (a, b) in enumerate(((gfil, gfil_ref), (gskip, gskip_ref), (gtaps, gtaps_ref)))
+    ]
+    results[0].start()
+    results[1].start()
 
     wait_all(tg_in, S - 1, tg_recv)
     share = LANES // C
@@ -526,12 +535,15 @@
             low = jnp.where(owner == q, shift(block, q * C), low)
             high = jnp.where(owner == q, shift(block, (q - 1) * C), high)
         lanes = slice(w * LANES, (w + 1) * LANES)
-        gtaps_ref[0, :, lanes] = low[0:3]
-        gtaps_ref[1, 0:2, lanes] = low[3:5]
-        gtaps_ref[1, 2:3, lanes] = high[0:1]
-        gtaps_ref[2, :, lanes] = high[1:4]
-
+        gtaps[0, :, lanes] = low[0:3]
+        gtaps[1, 0:2, lanes] = low[3:5]
+        gtaps[1, 2:3, lanes] = high[0:1]
+        gtaps[2, :, lanes] = high[1:4]
+
+    results[2].start()
     own_out.wait()
+    for copy in results:
+        copy.wait()
     wait_all(outb, S - 1, out_recv)
     wait_all(tok, S - 1, tok_send)
     wait_all(cot, S - 1, cot_send)
@@ -561,7 +573,6 @@
     K1 = S + 1
     forward, inverse, twist_cos, twist_sin = (jnp.asarray(t) for t in tables(S))
     any_spec = pl.BlockSpec(memory_space=pl.ANY)
-    vmem = pl.BlockSpec(memory_space=pltpu.VMEM)
     tile = (S, C, LANES)
     spectrum = (K1, C, 2 * LANES)
     dma = lambda n: pltpu.SemaphoreType.DMA((n,))
@@ -596,7 +607,11 @@
         pltpu.VMEM((DP, 5, LANES), F32),
         pltpu.VMEM((5, LANES), F32),
         pltpu.VMEM((S, 5, LANES), F32),
-        dma(9),
+        pltpu.VMEM((8, length), F32),
+        pltpu.VMEM((1, 8), F32),
+        pltpu.VMEM((3, 3, D), F32),
+        pltpu.VMEM((1, C), F32),
+        dma(10),
     ] + [pltpu.SemaphoreType.DMA] * 13
     shapes = (
         jax.ShapeDtypeStruct((1, D, LANES), BF16),
@@ -607,8 +622,8 @@
     results = pl.pallas_call(
         functools.partial(kernel, S, DP),
         out_shape=shapes,
-        in_specs=[any_spec] * 4 + [vmem] + [any_spec] * 5,
-        out_specs=(any_spec, vmem, vmem, vmem),
+        in_specs=[any_spec] * 10,
+        out_specs=(any_spec,) * 4,
         scratch_shapes=scratch,
         compiler_params=pltpu.CompilerParams(
             collective_id=0, has_side_effects=True, vmem_limit_bytes=56 * 1024 * 1024

time: 49.9 us -> 46.7 us (0.936)
  Pallas kernels: 49.1 us -> 46 us
    pallas_call x1, Pallas kernels: 47.2 us -> 44 us  [shards(): pl.pallas_call(functools.partial(kernel, S, DP), out_shape=shapes, in_spe...]
where the time goes in v4:
time: 46.7 us; the launch traced here: 46.6 us
  Pallas kernels  46 us (99%)
  between operations  0.64 us (1%)
    pallas_call x1, Pallas kernels, shards(): pl.pallas_call(functools.partial(kernel, S, DP), out_shape=shapes, in_spe...  44 us
    pallas_call x1, Pallas kernels, shards(): pl.pallas_call(hand_over, out_shape=shapes, in_specs=[any_spec] * 4, out_...  1.94 us

profile of v4, /device:TPU:1, one launch (start us, length us, event | category | flops | bytes accessed | tf_op | source)
XLA Modules:
  0.0 46.6 jit_solution(933872454006777545)
XLA Ops:
  0.6 44.0 %shard_map.129 = (bf16[1,2048,128]{2,1,0:T(8,128)(2,1)}, f32[8,4096]{1,0:T(8,128)}, f32[1,8]{1,0:T(1,128)}, f32[3,3,2048]{2,1,0:T(4,128)}) custom-call(s32[1,128]{1,0:T(1,128)} %tok_in.1, bf16[512,2048]{1,0:T(8,128)(2,1)} %emb_in.1, f32[3,3,2048]{2,1,0:T(4,128)} %taps_in.1, f32[64,4096]{1,0:T(8,128)} %fil_in.1, f32[1,64]{1,0:T(1,128)} %bitcast.2, ...), custom_call_target="tpu_custom_call" | custom-call | flops 1937768448 | bytes 6291456 | tf_op jit(solution)/shard_map/pallas_call | solution.py:622
  44.7 1.9 %shard_map.130 = (bf16[1,2048,128]{2,1,0:T(8,128)(2,1)}, f32[8,4096]{1,0:T(8,128)}, f32[1,8]{1,0:T(1,128)}, f32[3,3,2048]{2,1,0:T(4,128)}) custom-call(bf16[1,2048,128]{2,1,0:T(8,128)(2,1)} %get-tuple-element.12.refs_0_, f32[8,4096]{1,0:T(8,128)} %get-tuple-element.13.refs_1_, f32[1,8]{1,0:T(1,128)} %get-tuple-element.14.refs_2_, ...), custom_call_target="tpu_custom_call" | custom-call | tf_op jit(solution)/shard_map/pallas_call | solution.py:636

commit v5 on v4

--- a/solution.py
+++ b/solution.py
@@ -233,10 +233,13 @@
             src_ref=tok_in, dst_ref=tok.at[me], send_sem=tok_send, recv_sem=tok_recv,
             device_id={"seq": peer}, device_id_type=MESH)
 
-    def cot_copy(peer):
+    HALVES = 2
+    H = C // HALVES
+
+    def cot_copy(peer, half):
         return pltpu.make_async_remote_copy(
-            src_ref=cot_in.at[0, pl.ds(pl.multiple_of(peer * C, C), C)],
-            dst_ref=cot.at[me], send_sem=cot_send, recv_sem=cot_recv,
+            src_ref=cot_in.at[0, pl.ds(pl.multiple_of(peer * C + half * H, H), H)],
+            dst_ref=cot.at[me, pl.ds(half * H, H)], send_sem=cot_send, recv_sem=cot_recv.at[half],
             device_id={"seq": peer}, device_id_type=MESH)
 
     def out_copy(peer):
@@ -267,11 +270,12 @@
 
     for step in steps:
         tok_copy(peer_at(step)).start()
-    for step in steps:
-        cot_copy(peer_at(step)).start()
-
-    def spread_stage(load_block):
-        @pl.loop(0, C // 8)
+    for half in range(HALVES):
+        for step in steps:
+            cot_copy(peer_at(step), half).start()
+
+    def spread_stage(load_block, first=0, last=C // 8):
+        @pl.loop(first, last)
         def _(group):
             rows = pl.ds(pl.multiple_of(group * 8, 8), 8)
 
@@ -290,8 +294,8 @@
 
             padded_real_dft(lambda n: load_block(n, rows), S, emit)
 
-    def gather_stage(source, store):
-        @pl.loop(0, C // 8)
+    def gather_stage(source, store, first=0, last=C // 8):
+        @pl.loop(first, last)
         def _(group):
             rows = pl.ds(pl.multiple_of(group * 8, 8), 8)
 
@@ -306,12 +310,12 @@
 
             store(group, rows, real_inverse(fetch, 2 * S, 1, S))
 
-    chunk = 11 if K1 % 11 == 0 else 3
+    chunk = next(c for c in (11, 3, 5) if K1 % c == 0)
 
     def matrix(value, table):
-        flat = value.reshape(chunk * C, 2 * LANES).astype(BF16)
+        flat = value.reshape(-1, 2 * LANES).astype(BF16)
         result = jnp.dot(flat, table[...], preferred_element_type=F32)
-        return result.reshape(chunk, C, 2 * LANES)
+        return result.reshape(value.shape)
 
     def halves(value):
         return value[..., :LANES], value[..., LANES:]
@@ -416,35 +420,7 @@
         outb.at[me], out_ref.at[0, pl.ds(pl.multiple_of(me * C, C), C)], own_sem)
     own_out.start()
 
-    wait_all(cot, S - 1, cot_recv)
-
-    sums = [[] for _ in range(10)]
-    for part in range(C // 16):
-        rows = pl.ds(part * 16, 16)
-
-        def back_block(n, carry):
-            cot_f = cot[n, rows].astype(F32)
-            back = (cot_f * stream[1, n, rows].astype(F32)).astype(BF16).astype(F32)
-            bak[n, rows] = back
-            grad = cot_f * resp[n, rows].astype(F32)
-            fresh = [grad * lag[i, n, rows].astype(F32) for i in range(3)] + [back * gat[n, rows]]
-            return tuple(a + b for a, b in zip(carry, fresh))
-
-        start = jnp.zeros((16, LANES), F32)
-        found = lax.fori_loop(0, S, back_block, (start,) * 4, unroll=16)
-        for j, value in zip((3, 4, 5, 9), found):
-            sums[j].append(value)
-
-    spread_stage(lambda n, rows: bak[n, rows])
-
-    @pl.loop(0, K1 // chunk)
-    def _(i):
-        part = pl.ds(i * chunk, chunk)
-        spectrum = matrix(work[part], wf)
-        bspec[part] = spectrum
-        br, bi = halves(spectrum)
-        gr, gi = halves(gspec[part])
-        inv[part] = matrix(joined(gr * br + gi * bi, gr * bi - gi * br), wi)
+    tile_zero = jnp.zeros((16, LANES), F32)
 
     def send_filter(group, rows, values):
         for m in range(S // 2):
@@ -455,44 +431,107 @@
         def _():
             rs_copy(group).start()
 
-    gather_stage(inv, send_filter)
-
-    @pl.loop(0, K1 // chunk)
-    def _(i):
-        part = pl.ds(i * chunk, chunk)
-        br, bi = halves(bspec[part])
-        fr, fi = halves(fspec[part])
-        inv[part] = matrix(joined(br * fr + bi * fi, bi * fr - br * fi), wi)
-
-    gather_stage(inv, keep)
-
-    for part in range(C // 16):
-        rows = pl.ds(part * 16, 16)
-        skip_part = skb[rows]
-
-        def grad_block(n, carry):
-            grad = (conv[n, rows] + skip_part * bak[n, rows]).astype(BF16).astype(F32)
-            grad_first = grad * stream[2, n, rows].astype(F32)
-            grad_value = grad * stream[0, n, rows].astype(F32)
-            lags = [lag[i, n, rows].astype(F32) for i in range(3)]
-            fresh = [grad_first * one for one in lags] + [grad_value * one for one in lags]
-            return tuple(a + b for a, b in zip(carry, fresh))
-
-        start = jnp.zeros((16, LANES), F32)
-        found = lax.fori_loop(0, S, grad_block, (start,) * 6, unroll=16)
-        for j, value in zip((0, 1, 2, 6, 7, 8), found):
-            sums[j].append(value)
-
-    def placed(j, shift):
-        total = jnp.sum(jnp.concatenate(sums[j], axis=0), axis=1, keepdims=True)
-        spot = lane_id == lax.broadcasted_iota(jnp.int32, (C, LANES), 0) + shift
-        kept = jnp.where(spot, jnp.broadcast_to(total, (C, LANES)), 0.0)
-        return jnp.sum(kept, axis=0, keepdims=True)
-
-    tp_out[...] = jnp.concatenate([placed(j, 0) + placed(j + 5, C) for j in range(5)], axis=0)
+    sums = [[[] for _ in range(10)] for _ in range(HALVES)]
+
+    def span(half):
+        return pl.ds(half * H, H), (half * H // 8, (half + 1) * H // 8)
+
+    def back_spectrum(half):
+        held, groups = span(half)
+        arrived = cot.at[pl.ds(0, S - 1), held]
+        pltpu.make_async_copy(arrived, arrived, cot_recv.at[half]).wait()
+
+        for first in range(half * H, (half + 1) * H, 16):
+            rows = pl.ds(first, 16)
+
+            def back_block(n, carry):
+                cot_f = cot[n, rows].astype(F32)
+                back = (cot_f * stream[1, n, rows].astype(F32)).astype(BF16).astype(F32)
+                bak[n, rows] = back
+                grad = cot_f * resp[n, rows].astype(F32)
+                fresh = [grad * lag[i, n, rows].astype(F32) for i in range(3)] + [back * gat[n, rows]]
+                return tuple(a + b for a, b in zip(carry, fresh))
+
+            found = lax.fori_loop(0, S, back_block, (tile_zero,) * 4, unroll=16)
+            for j, value in zip((3, 4, 5, 9), found):
+                sums[half][j].append(value)
+
+        spread_stage(lambda n, rows: bak[n, rows], *groups)
+
+        @pl.loop(0, K1 // chunk)
+        def _(i):
+            part = pl.ds(i * chunk, chunk)
+            bspec[part, held] = matrix(work[part, held], wf)
+
+    def filter_part(half):
+        held, groups = span(half)
+
+        @pl.loop(0, K1 // chunk)
+        def _(i):
+            part = pl.ds(i * chunk, chunk)
+            br, bi = halves(bspec[part, held])
+            gr, gi = halves(gspec[part, held])
+            inv[part, held] = matrix(joined(gr * br + gi * bi, gr * bi - gi * br), wi)
+
+        gather_stage(inv, send_filter, *groups)
+
+    def signal_part(half):
+        held, groups = span(half)
+
+        @pl.loop(0, K1 // chunk)
+        def _(i):
+            part = pl.ds(i * chunk, chunk)
+            br, bi = halves(bspec[part, held])
+            fr, fi = halves(fspec[part, held])
+            inv[part, held] = matrix(joined(br * fr + bi * fi, bi * fr - br * fi), wi)
+
+        gather_stage(inv, keep, *groups)
+
+        for first in range(half * H, (half + 1) * H, 16):
+            rows = pl.ds(first, 16)
+            skip_part = skb[rows]
+
+            def grad_block(n, carry):
+                grad = (conv[n, rows] + skip_part * bak[n, rows]).astype(BF16).astype(F32)
+                grad_first = grad * stream[2, n, rows].astype(F32)
+                grad_value = grad * stream[0, n, rows].astype(F32)
+                lags = [lag[i, n, rows].astype(F32) for i in range(3)]
+                fresh = [grad_first * one for one in lags] + [grad_value * one for one in lags]
+                return tuple(a + b for a, b in zip(carry, fresh))
+
+            found = lax.fori_loop(0, S, grad_block, (tile_zero,) * 6, unroll=16)
+            for j, value in zip((0, 1, 2, 6, 7, 8), found):
+                sums[half][j].append(value)
+
+    def packed(half):
+        lane = lax.broadcasted_iota(jnp.int32, (H, LANES), 1)
+        channel = lax.broadcasted_iota(jnp.int32, (H, LANES), 0) + half * H
+
+        def spread(j):
+            total = jnp.sum(jnp.concatenate(sums[half][j], axis=0), axis=1, keepdims=True)
+            return jnp.broadcast_to(total, (H, LANES))
+
+        return jnp.concatenate([
+            jnp.sum(
+                jnp.where(lane == channel, spread(j), jnp.where(lane == channel + C, spread(j + 5), 0.0)),
+                axis=0, keepdims=True)
+            for j in range(5)
+        ], axis=0)
+
+    last = HALVES - 1
+    for half in range(last):
+        back_spectrum(half)
+        filter_part(half)
+        signal_part(half)
+        early = packed(half)
+        tp_out[...] = early if half == 0 else tp_out[...] + early
+    back_spectrum(last)
+    signal_part(last)
+    tp_out[...] = tp_out[...] + packed(last)
     for k in range(1, DP):
         tp_copy(dp_at(k)).start()
     tp_in[mine] = tp_out[...]
+    filter_part(last)
 
     wait_all(tp_in, DP - 1, tp_recv)
     total = tp_in[0]
@@ -612,7 +651,7 @@
         pltpu.VMEM((3, 3, D), F32),
         pltpu.VMEM((1, C), F32),
         dma(10),
-    ] + [pltpu.SemaphoreType.DMA] * 13
+    ] + [pltpu.SemaphoreType.DMA] * 4 + [dma(2)] + [pltpu.SemaphoreType.DMA] * 8
     shapes = (
         jax.ShapeDtypeStruct((1, D, LANES), BF16),
         jax.ShapeDtypeStruct((8, length), F32),

time: 46.7 us -> 43.5 us (0.931)
  Pallas kernels: 46 us -> 42.7 us
    pallas_call x1, Pallas kernels: 44 us -> 40.8 us  [shards(): pl.pallas_call(functools.partial(kernel, S, DP), out_shape=shapes, in_spe...]
where the time goes in v5:
time: 43.5 us; the launch traced here: 43.3 us
  Pallas kernels  42.7 us (98%)
  between operations  0.64 us (1%)
    pallas_call x1, Pallas kernels, shards(): pl.pallas_call(functools.partial(kernel, S, DP), out_shape=shapes, in_spe...  40.8 us
    pallas_call x1, Pallas kernels, shards(): pl.pallas_call(hand_over, out_shape=shapes, in_specs=[any_spec] * 4, out_...  1.94 us

profile of v5, /device:TPU:1, one launch (start us, length us, event | category | flops | bytes accessed | tf_op | source)
XLA Modules:
  0.0 43.3 jit_solution(9118682161243555106)
XLA Ops:
  0.6 40.8 %shard_map.129 = (bf16[1,2048,128]{2,1,0:T(8,128)(2,1)}, f32[8,4096]{1,0:T(8,128)}, f32[1,8]{1,0:T(1,128)}, f32[3,3,2048]{2,1,0:T(4,128)}) custom-call(s32[1,128]{1,0:T(1,128)} %tok_in.1, bf16[512,2048]{1,0:T(8,128)(2,1)} %emb_in.1, f32[3,3,2048]{2,1,0:T(4,128)} %taps_in.1, f32[64,4096]{1,0:T(8,128)} %fil_in.1, f32[1,64]{1,0:T(1,128)} %bitcast.2, ...), custom_call_target="tpu_custom_call" | custom-call | flops 1937768448 | bytes 6291456 | tf_op jit(solution)/shard_map/pallas_call | solution.py:661
  41.4 1.9 %shard_map.130 = (bf16[1,2048,128]{2,1,0:T(8,128)(2,1)}, f32[8,4096]{1,0:T(8,128)}, f32[1,8]{1,0:T(1,128)}, f32[3,3,2048]{2,1,0:T(4,128)}) custom-call(bf16[1,2048,128]{2,1,0:T(8,128)(2,1)} %get-tuple-element.12.refs_0_, f32[8,4096]{1,0:T(8,128)} %get-tuple-element.13.refs_1_, f32[1,8]{1,0:T(1,128)} %get-tuple-element.14.refs_2_, ...), custom_call_target="tpu_custom_call" | custom-call | tf_op jit(solution)/shard_map/pallas_call | solution.py:675

commit v6 on v5

--- a/solution.py
+++ b/solution.py
@@ -327,7 +327,7 @@
         loads[i].wait()
     spread_stage(lambda n, rows: fil[rows, n * LANES : (n + 1) * LANES])
 
-    @pl.loop(0, K1 // chunk)
+    @pl.loop(0, K1 // chunk, unroll=3)
     def _(i):
         part = pl.ds(i * chunk, chunk)
         fspec[part] = matrix(work[part], wf)
@@ -380,11 +380,11 @@
         return (before1, before2)
 
     zero = jnp.zeros((C, LANES), F32)
-    lax.fori_loop(0, S // 2, stream_pair, (zero, zero), unroll=4)
+    lax.fori_loop(0, S // 2, stream_pair, (zero, zero), unroll=8)
 
     spread_stage(lambda n, rows: gat[n, rows])
 
-    @pl.loop(0, K1 // chunk)
+    @pl.loop(0, K1 // chunk, unroll=3)
     def _(i):
         part = pl.ds(i * chunk, chunk)
         spectrum = matrix(work[part], wf)
@@ -458,7 +458,7 @@
 
         spread_stage(lambda n, rows: bak[n, rows], *groups)
 
-        @pl.loop(0, K1 // chunk)
+        @pl.loop(0, K1 // chunk, unroll=3)
         def _(i):
             part = pl.ds(i * chunk, chunk)
             bspec[part, held] = matrix(work[part, held], wf)
@@ -466,7 +466,7 @@
     def filter_part(half):
         held, groups = span(half)
 
-        @pl.loop(0, K1 // chunk)
+        @pl.loop(0, K1 // chunk, unroll=3)
         def _(i):
             part = pl.ds(i * chunk, chunk)
             br, bi = halves(bspec[part, held])
@@ -478,7 +478,7 @@
     def signal_part(half):
         held, groups = span(half)
 
-        @pl.loop(0, K1 // chunk)
+        @pl.loop(0, K1 // chunk, unroll=3)
         def _(i):
             part = pl.ds(i * chunk, chunk)
             br, bi = halves(bspec[part, held])

time: 43.5 us -> 42.3 us (0.972)
  Pallas kernels: 42.7 us -> 41.6 us
    pallas_call x1, Pallas kernels: 40.8 us -> 39.6 us  [shards(): pl.pallas_call(functools.partial(kernel, S, DP), out_shape=shapes, in_spe...]
where the time goes in v6:
time: 42.3 us; the launch traced here: 42.2 us
  Pallas kernels  41.6 us (98%)
  between operations  0.64 us (2%)
    pallas_call x1, Pallas kernels, shards(): pl.pallas_call(functools.partial(kernel, S, DP), out_shape=shapes, in_spe...  39.6 us
    pallas_call x1, Pallas kernels, shards(): pl.pallas_call(hand_over, out_shape=shapes, in_specs=[any_spec] * 4, out_...  1.94 us

profile of v6, /device:TPU:1, one launch (start us, length us, event | category | flops | bytes accessed | tf_op | source)
XLA Modules:
  0.0 42.2 jit_solution(11747776692499987934)
XLA Ops:
  0.6 39.6 %shard_map.129 = (bf16[1,2048,128]{2,1,0:T(8,128)(2,1)}, f32[8,4096]{1,0:T(8,128)}, f32[1,8]{1,0:T(1,128)}, f32[3,3,2048]{2,1,0:T(4,128)}) custom-call(s32[1,128]{1,0:T(1,128)} %tok_in.1, bf16[512,2048]{1,0:T(8,128)(2,1)} %emb_in.1, f32[3,3,2048]{2,1,0:T(4,128)} %taps_in.1, f32[64,4096]{1,0:T(8,128)} %fil_in.1, f32[1,64]{1,0:T(1,128)} %bitcast.2, ...), custom_call_target="tpu_custom_call" | custom-call | flops 1937768448 | bytes 6291456 | tf_op jit(solution)/shard_map/pallas_call | solution.py:661
  40.3 1.9 %shard_map.130 = (bf16[1,2048,128]{2,1,0:T(8,128)(2,1)}, f32[8,4096]{1,0:T(8,128)}, f32[1,8]{1,0:T(1,128)}, f32[3,3,2048]{2,1,0:T(4,128)}) custom-call(bf16[1,2048,128]{2,1,0:T(8,128)(2,1)} %get-tuple-element.12.refs_0_, f32[8,4096]{1,0:T(8,128)} %get-tuple-element.13.refs_1_, f32[1,8]{1,0:T(1,128)} %get-tuple-element.14.refs_2_, ...), custom_call_target="tpu_custom_call" | custom-call | tf_op jit(solution)/shard_map/pallas_call | solution.py:675
